TPU v7x, 128 devices: a whole 4x4x4 slice. The times are simulated.
128 devices in a mesh: blk: 16 (over x, y), sub: 8 (over z, core).
Axes of the slice: x: 4, y: 4, z: 4, core: 2. Of those that a mesh axis runs over, the one named last changes fastest.
Arguments:
- u_flow: float32 [16, 4096, 4096], P(None, 'blk', 'sub'), may hold values from -60 to 60
- v_flow: float32 [16, 4096, 4096], P(None, 'blk', 'sub'), may hold values from -60 to 60
- thickness: float32 [16], replicated, may hold values from 0.1 to 0.5
- depth_levels: int32 [4096, 4096], P('blk', 'sub'), may hold values from 1 to 16
- block_ocean: int32 [32, 32], replicated, may hold values from 0 to 1, as said below
- coef_x: float32 [4096, 4096], P('blk', 'sub'), may hold values from 0.2 to 1
- coef_y: float32 [4096, 4096], P('blk', 'sub'), may hold values from 0.2 to 1
- coef_xy: float32 [4096, 4096], P('blk', 'sub'), may hold values from 0.2 to 1
- coef_xm: float32 [4096, 4096], P('blk', 'sub'), may hold values from 0.2 to 1
- extra_diagonal: float32 [4096, 4096], P('blk', 'sub'), may hold values from 0.02 to 2
Outputs:
- surface_height: float32 [4096, 4096], P('blk', 'sub')
- residual: float32 [4096, 4096], P('blk', 'sub')
Inputs may be any that keep to these rules, and one draw needn't show every extreme that they name: `block_ocean`: in every band of 256 rows of cells that one index of blk holds, exactly three quarters of the blocks are ocean blocks.
All inputs are finite; a program needn't handle non-finite values.
Results may differ from a plain program's by a relative error of at most 0.0003.
Values sent between devices are 32-bit elements; how exact they have to be, the bound alone decides.
A program may use at most 128 MiB of HBM per device.

v0:
```python
import jax
import jax.numpy as jnp
from jax import lax
from jax.sharding import PartitionSpec as P

BLOCK = 128
ITERS = 4


OFFSETS = ((1, 0), (-1, 0), (0, 1), (0, -1), (1, 1), (-1, -1), (1, -1), (-1, 1))


def padded_2(value, sides, width):
    for axis, dim in sides:
        peers, length = (lax.axis_size(axis), value.shape[dim])
        up = [(i, (i + 1) % peers) for i in range(peers - 1)]
        down = [(j, i) for i, j in up]
        last = lax.slice_in_dim(value, length - width, length, axis=dim)
        initial = lax.slice_in_dim(value, 0, width, axis=dim)
        before = lax.ppermute(last, axis, up)
        after = lax.ppermute(initial, axis, down)
        value = jnp.concatenate([before, value, after], axis=dim)
    return value


def column_sums(u_flow, v_flow, thickness, depth_levels, ocean_mask):

    def add_level(level_index, totals):
        active = (depth_levels > level_index).astype(jnp.float32) * thickness[level_index]
        return (totals[0] + active * u_flow[level_index], totals[1] + active * v_flow[level_index])

    empty = jnp.zeros(depth_levels.shape, jnp.float32)
    flux_u, flux_v = lax.fori_loop(0, u_flow.shape[0], add_level, (empty, empty))
    return (ocean_mask * flux_u, ocean_mask * flux_v)


def neighbour_weights(padded):
    return [
        padded[0, ..., 1:-1, 1:-1],
        padded[0, ..., :-2, 1:-1],
        padded[1, ..., 1:-1, 1:-1],
        padded[1, ..., 1:-1, :-2],
        padded[2, ..., 1:-1, 1:-1],
        padded[2, ..., :-2, :-2],
        padded[3, ..., 1:-1, 1:-1],
        padded[3, ..., :-2, 2:],
    ]


def center_of(weights, extra_diagonal):
    center = extra_diagonal
    for weight in weights:
        center = center + weight
    return center


def operate(padded_field, weights, center, ocean_mask):
    row_count, col_count = center.shape[-2:]
    beside = jnp.zeros(center.shape, jnp.float32)
    for offset, weight in zip(OFFSETS, weights):
        beside = (
            beside
            + weight
            * padded_field[
                ...,
                1 + offset[0] : 1 + offset[0] + row_count,
                1 + offset[1] : 1 + offset[1] + col_count,
            ]
        )
    return ocean_mask * (center * padded_field[..., 1:-1, 1:-1] - beside)


def chron_gear(forcing, inverse, apply_operator):
    surface_height = jnp.zeros(forcing.shape, jnp.float32)
    residual = forcing
    search = jnp.zeros(forcing.shape, jnp.float32)
    search_image = jnp.zeros(forcing.shape, jnp.float32)
    rho_old = jnp.float32(1.0)
    sigma_value = jnp.float32(0.0)
    for iteration in range(ITERS):
        scaled = residual * inverse
        applied = apply_operator(scaled)
        rho_now, curvature = lax.psum(
            (jnp.sum(residual * scaled), jnp.sum(scaled * applied)), ("blk", "sub")
        )
        beta_ratio = rho_now / rho_old
        sigma_value = curvature - beta_ratio * beta_ratio * sigma_value
        alpha_step = rho_now / sigma_value
        rho_old = rho_now
        search = scaled + beta_ratio * search
        search_image = applied + beta_ratio * search_image
        surface_height = surface_height + alpha_step * search
        residual = residual - alpha_step * search_image
    return (surface_height, residual)


def body(
    u_flow,
    v_flow,
    thickness,
    depth_levels,
    block_ocean,
    coef_x,
    coef_y,
    coef_xy,
    coef_xm,
    extra_diagonal,
):
    row_count, col_count = depth_levels.shape
    block_rows = row_count // BLOCK
    block_cols = col_count // BLOCK
    blk_index = lax.axis_index("blk")
    sub_index = lax.axis_index("sub")
    tile_blocks = lax.dynamic_slice(
        block_ocean, (blk_index * block_rows, sub_index * block_cols), (block_rows, block_cols)
    )
    ocean_mask = jnp.repeat(jnp.repeat(tile_blocks, BLOCK, axis=0), BLOCK, axis=1).astype(
        jnp.float32
    )
    flux_u, flux_v = column_sums(u_flow, v_flow, thickness, depth_levels, ocean_mask)
    padded_flux = padded_2(jnp.stack([flux_u, flux_v]), (("blk", 1), ("sub", 2)), 1)
    forcing = ocean_mask * (
        0.5
        * (
            padded_flux[0, 2:, 1:-1]
            - padded_flux[0, :-2, 1:-1]
            + (padded_flux[1, 1:-1, 2:] - padded_flux[1, 1:-1, :-2])
        )
    )
    padded_coefs = padded_2(
        jnp.stack([coef_x, coef_y, coef_xy, coef_xm]), (("blk", 1), ("sub", 2)), 1
    )
    weights = neighbour_weights(padded_coefs)
    center = center_of(weights, extra_diagonal)
    inverse = 1.0 / center

    def apply_tiles(scaled):
        widened = padded_2(scaled, (("blk", 0), ("sub", 1)), 1)
        return operate(widened, weights, center, ocean_mask)

    return chron_gear(forcing, inverse, apply_tiles)


def solution(mesh):
    placed = (
        P(None, "blk", "sub"),
        P(None, "blk", "sub"),
        P(),
        P("blk", "sub"),
        P(),
        P("blk", "sub"),
        P("blk", "sub"),
        P("blk", "sub"),
        P("blk", "sub"),
        P("blk", "sub"),
    )
    return jax.shard_map(
        body,
        mesh=mesh,
        in_specs=placed,
        out_specs=(P("blk", "sub"), P("blk", "sub")),
        check_vma=False,
    )
```

profile of v0, /device:TPU:1, one launch (start us, length us, event | category | flops | bytes accessed | tf_op | source)
XLA Modules:
  0.0 499.3 jit_solution(10220817590169575644)
XLA Ops:
  4.6 2.0 pad_maximum_fusion.1
  8.0 4.0 collective-permute-start.4
  13.3 69.3 %while.16 = (s32[]{:T(128)}, f32[256,512]{1,0:T(8,128)S(1)}, f32[256,512]{1,0:T(8,128)S(1)}, s32[256,512]{1,0:T(8,128)S(1)}, f32[16]{0:T(128)S(1)}, /*index=5*/f...) while((s32[]{:T(128)}, f32[256,512]{1,0:T(8,128)S(1)}, ...), condition=%wide.region_1.0_spmd.clone, body=%wide.region_0.0_spmd.clone.sunk | while | flops 1179651 | bytes 3933820 | solution.py:33
  13.9 1.9 fusion.67
  15.8 1.8 fusion.68
  18.2 1.9 fusion.67
  20.1 1.8 fusion.68
  22.5 1.9 fusion.67
  24.5 1.8 fusion.68
  26.9 1.9 fusion.67
  28.8 1.8 fusion.68
  31.2 1.9 fusion.67
  33.1 1.8 fusion.68
  35.5 1.9 fusion.67
  37.5 1.8 fusion.68
  39.9 1.9 fusion.67
  41.8 1.8 fusion.68
  44.2 1.9 fusion.67
  46.1 1.8 fusion.68
  48.5 1.9 fusion.67
  50.4 1.8 fusion.68
  52.9 1.9 fusion.67
  54.8 1.8 fusion.68
  57.2 1.9 fusion.67
  59.1 1.8 fusion.68
  61.5 1.9 fusion.67
  65.8 1.9 fusion.67
  70.2 1.9 fusion.67
  72.1 1.8 fusion.68
  74.5 1.9 fusion.67
  78.8 1.9 fusion.67
  80.7 1.8 fusion.68
  86.1 4.6 collective-permute-start.1
  90.8 2.0 copy.48
  92.8 2.0 pad_maximum_fusion
  99.0 3.4 collective-permute-start.7
  103.3 1.9 collective-permute-start.2
  105.2 3.8 collective-permute-start.3
  109.0 3.7 copy.51
  113.0 2.4 collective-permute-start.6
  116.6 11.5 %pad_maximum_fusion.14 = f32[1,256,512]{2,0,1:T(1,128)S(1)} fusion(f32[4,258,1]{2,0,1:T(4,128)} %copy.53, f32[4,1,512]{2,0,1:T(4,128)S(1)} %collective-permute-done.5, f32[4,1,512]{2,0,1:T(4,128)S(1)} %collective-permute-done.4, f32[1,256,512]{2,0,1:T(1,128)} %copy-done.37, f32[1,256,512]{2,0,1:T(1,128)} %copy-done.35, f32[1,256,512]{2,0,1:T(1,128)} %copy-done.33, ...), kind=kLoop, calls=%fused_computation.96 | loop fusion | flops 786432 | bytes 2641952 | tf_op jit(solution)/shard_map/concatenate | solution.py:22
  129.1 3.9 fusion.55
  134.5 4.3 collective-permute-start.9
  139.6 3.0 collective-permute-start.10
  142.6 3.4 collective-permute-start.11
  148.3 2.5 multiply_reduce_fusion.6
  150.8 72.9 %all-reduce.3 = (f32[]{:T(128)}, f32[]{:T(128)}) all-reduce(f32[]{:T(128)} %get-tuple-element.162, f32[]{:T(128)} %get-tuple-element.161), channel_id=1, replica_groups=mesh['blk'=16,'sub'=8] {'blk','sub'}, use_global_device_ids=true, to_apply=%region_3.0 | all-reduce | flops 2 | bytes 16 | tf_op jit(solution)/shard_map/psum | solution.py:83
  230.2 4.0 collective-permute-start.13
  235.0 3.7 collective-permute-start.14
  238.7 3.5 collective-permute-start.15
  244.6 2.4 multiply_reduce_fusion.4
  247.0 66.7 %all-reduce.2 = (f32[]{:T(128)}, f32[]{:T(128)}) all-reduce(f32[]{:T(128)} %get-tuple-element.160, f32[]{:T(128)} %get-tuple-element.159), channel_id=1, replica_groups=mesh['blk'=16,'sub'=8] {'blk','sub'}, use_global_device_ids=true, to_apply=%region_7.0 | all-reduce | flops 2 | bytes 16 | tf_op jit(solution)/shard_map/psum | solution.py:83
  316.4 2.5 fusion.53
  320.6 4.0 collective-permute-start.17
  325.4 3.7 collective-permute-start.18
  329.1 2.9 collective-permute-start.19
  334.3 2.4 multiply_reduce_fusion.2
  336.7 67.1 %all-reduce.1 = (f32[]{:T(128)}, f32[]{:T(128)}) all-reduce(f32[]{:T(128)} %get-tuple-element.158, f32[]{:T(128)} %get-tuple-element.157), channel_id=1, replica_groups=mesh['blk'=16,'sub'=8] {'blk','sub'}, use_global_device_ids=true, to_apply=%region_11.0 | all-reduce | flops 2 | bytes 16 | tf_op jit(solution)/shard_map/psum | solution.py:83
  409.9 4.0 collective-permute-start.21
  414.8 4.0 collective-permute-start.22
  418.7 1.9 collective-permute-start.23
  423.0 2.4 multiply_reduce_fusion
  425.4 67.5 %all-reduce = (f32[]{:T(128)}, f32[]{:T(128)}) all-reduce(f32[]{:T(128)} %get-tuple-element.156, f32[]{:T(128)} %get-tuple-element.155), channel_id=1, replica_groups=mesh['blk'=16,'sub'=8] {'blk','sub'}, use_global_device_ids=true, to_apply=%region_15.0 | all-reduce | flops 2 | bytes 16 | tf_op jit(solution)/shard_map/psum | solution.py:83
  495.7 3.6 multiply_subtract_fusion
  (172 shorter events, 53.6 us)
Async XLA Ops:
  0.6 3.1 copy-start.1
  0.6 3.5 copy-start
  2.1 4.4 copy-start.31
  4.5 3.4 copy-start.37
  4.5 8.8 %copy-start.9 = (s32[256,512]{1,0:T(8,128)S(1)}, s32[256,512]{1,0:T(8,128)}, u32[]{:S(2)}) copy-start(s32[256,512]{1,0:T(8,128)} %param.15) | copy-start | bytes 1572868
  4.6 8.8 %copy-start.44 = (f32[16]{0:T(128)S(1)}, f32[16]{0:T(128)}, u32[]{:S(2)}) copy-start(f32[16]{0:T(128)} %param.14) | copy-start | bytes 196
  8.0 84.8 %collective-permute-start.4 = (f32[4,1,512]{2,0,1:T(4,128)S(1)}, f32[4,1,512]{2,0,1:T(4,128)S(1)}, u32[]{:S(2)}, u32[]{:S(2)}) collective-permute-start(f32[4,1,512]{2,0,1:T(4,128)S(1)} %get-tuple-element.206), channel_id=1, source_target_pairs={{0,8},{8,16},{16,24},{24,32},{32,40},{40,48},{48,56},{56,64},{64,7... | collective-permute-start | bytes 24584 | tf_op jit(solution)/shard_map/ppermute | solution.py:20
  12.0 80.8 %collective-permute-start.5 = (f32[4,1,512]{2,0,1:T(4,128)S(1)}, f32[4,1,512]{2,0,1:T(4,128)S(1)}, u32[]{:S(2)}, u32[]{:S(2)}) collective-permute-start(f32[4,1,512]{2,0,1:T(4,128)S(1)} %get-tuple-element.207), channel_id=1, source_target_pairs={{8,0},{16,8},{24,16},{32,24},{40,32},{48,40},{56,48},{64,56},{72,6... | collective-permute-start | bytes 24584 | tf_op jit(solution)/shard_map/ppermute | solution.py:21
  83.4 7.4 %copy-start.27 = (f32[4,256,512]{2,0,1:T(4,128)S(1)}, f32[4,256,512]{2,0,1:T(4,128)}, u32[]{:S(2)}) copy-start(f32[4,256,512]{2,0,1:T(4,128)} %copy-done.26) | copy-start | bytes 6291460
  83.9 18.5 %copy-start.28 = (f32[1,256,512]{2,1,0:T(8,128)}, f32[1,256,512]{2,1,0:T(8,128)S(1)}, u32[]{:S(2)}) copy-start(f32[1,256,512]{2,1,0:T(8,128)S(1)} %get-tuple-element.236) | copy-start | bytes 1572868
  84.7 8.1 %copy-start.32 = (f32[1,256,512]{2,0,1:T(1,128)S(1)}, f32[1,256,512]{2,0,1:T(1,128)}, u32[]{:S(2)}) copy-start(f32[1,256,512]{2,0,1:T(1,128)} %copy-done.31) | copy-start | bytes 1572868
  84.7 8.1 %copy-start.34 = (f32[1,256,512]{2,0,1:T(1,128)S(1)}, f32[1,256,512]{2,0,1:T(1,128)}, u32[]{:S(2)}) copy-start(f32[1,256,512]{2,0,1:T(1,128)} %copy-done.33) | copy-start | bytes 1572868
  84.7 8.1 %copy-start.36 = (f32[1,256,512]{2,0,1:T(1,128)S(1)}, f32[1,256,512]{2,0,1:T(1,128)}, u32[]{:S(2)}) copy-start(f32[1,256,512]{2,0,1:T(1,128)} %copy-done.35) | copy-start | bytes 1572868
  84.7 8.1 %copy-start.38 = (f32[1,256,512]{2,0,1:T(1,128)S(1)}, f32[1,256,512]{2,0,1:T(1,128)}, u32[]{:S(2)}) copy-start(f32[1,256,512]{2,0,1:T(1,128)} %copy-done.37) | copy-start | bytes 1572868
  84.7 17.7 %collective-permute-start = (f32[2,1,512]{2,1,0:T(1,128)S(1)}, f32[2,1,512]{2,1,0:T(1,128)S(1)}, u32[]{:S(2)}, u32[]{:S(2)}) collective-permute-start(f32[2,1,512]{2,1,0:T(1,128)S(1)} %get-tuple-element.211), channel_id=1, source_target_pairs={{8,0},{16,8},{24,16},{32,24},{40,32},{48,40},{56,48},{64,56},{72,6... | collective-permute-start | bytes 12296 | tf_op jit(solution)/shard_map/ppermute | solution.py:21
  86.1 16.3 %collective-permute-start.1 = (f32[2,1,512]{2,1,0:T(1,128)S(1)}, f32[2,1,512]{2,1,0:T(1,128)S(1)}, u32[]{:S(2)}, u32[]{:S(2)}) collective-permute-start(f32[2,1,512]{2,1,0:T(1,128)S(1)} %get-tuple-element.210), channel_id=1, source_target_pairs={{0,8},{8,16},{16,24},{24,32},{32,40},{40,48},{48,56},{56,64},{64,7... | collective-permute-start | bytes 12296 | tf_op jit(solution)/shard_map/ppermute | solution.py:20
  96.3 6.2 %copy-start.30 = (f32[1,256,512]{2,1,0:T(8,128)S(1)}, f32[1,256,512]{2,1,0:T(8,128)}, u32[]{:S(2)}) copy-start(f32[1,256,512]{2,1,0:T(8,128)} %copy-done.29) | copy-start | bytes 1572868
  99.0 16.5 %collective-permute-start.7 = (f32[4,258,1]{1,0,2:T(4,128)S(1)}, f32[4,258,1]{1,0,2:T(4,128)S(1)}, u32[]{:S(2)}, u32[]{:S(2)}) collective-permute-start(f32[4,258,1]{1,0,2:T(4,128)S(1)} %copy.52), channel_id=1, source_target_pairs={{1,0},{2,1},{3,2},{4,3},{5,4},{6,5},{7,6},{9,8},{10,9},{11,10},{12... | collective-permute-start | bytes 12392 | tf_op jit(solution)/shard_map/ppermute | solution.py:21
  103.3 25.8 %collective-permute-start.2 = (f32[2,258,1]{2,1,0:T(8,128)}, f32[2,258,1]{2,1,0:T(8,128)S(1)}, u32[]{:S(2)}, u32[]{:S(2)}) collective-permute-start(f32[2,258,1]{2,1,0:T(8,128)} %get-tuple-element.208), channel_id=1, source_target_pairs={{1,0},{2,1},{3,2},{4,3},{5,4},{6,5},{7,6},{9,8},{10,9},{11,10},{12... | collective-permute-start | bytes 6200 | tf_op jit(solution)/shard_map/ppermute | solution.py:21
  105.2 7.5 %copy-start.43 = (f32[4,258,1]{2,0,1:T(4,128)S(1)}, f32[4,258,1]{2,0,1:T(4,128)}, u32[]{:S(2)}) copy-start(f32[4,258,1]{2,0,1:T(4,128)} %get-tuple-element.204) | copy-start | bytes 12388
  105.2 23.9 %collective-permute-start.3 = (f32[2,258,1]{2,1,0:T(8,128)}, f32[2,258,1]{2,1,0:T(8,128)}, u32[]{:S(2)}, u32[]{:S(2)}) collective-permute-start(f32[2,258,1]{2,1,0:T(8,128)} %get-tuple-element.209), channel_id=1, source_target_pairs={{0,1},{1,2},{2,3},{3,4},{4,5},{5,6},{6,7},{8,9},{9,10},{10,11},{11... | collective-permute-start | bytes 6200 | tf_op jit(solution)/shard_map/ppermute | solution.py:20
  113.0 15.1 %collective-permute-start.6 = (f32[4,258,1]{1,0,2:T(4,128)S(1)}, f32[4,258,1]{1,0,2:T(4,128)S(1)}, u32[]{:S(2)}, u32[]{:S(2)}) collective-permute-start(f32[4,258,1]{1,0,2:T(4,128)S(1)} %copy.49), channel_id=1, source_target_pairs={{0,1},{1,2},{2,3},{3,4},{4,5},{5,6},{6,7},{8,9},{9,10},{10,11},{11... | collective-permute-start | bytes 12392 | tf_op jit(solution)/shard_map/ppermute | solution.py:20
  115.4 13.7 %copy-start.2 = (f32[256,512]{1,0:T(8,128)S(1)}, f32[256,512]{1,0:T(8,128)}, u32[]{:S(2)}) copy-start(f32[256,512]{1,0:T(8,128)} %param.18) | copy-start | bytes 1572868
  115.4 13.7 %copy-start.3 = (f32[256,512]{1,0:T(8,128)S(1)}, f32[256,512]{1,0:T(8,128)}, u32[]{:S(2)}) copy-start(f32[256,512]{1,0:T(8,128)} %param.17) | copy-start | bytes 1572868
  133.0 17.8 %copy-start.5 = (f32[256,512]{1,0:T(8,128)}, f32[256,512]{1,0:T(8,128)S(1)}, u32[]{:S(2)}) copy-start(f32[256,512]{1,0:T(8,128)S(1)} %get-tuple-element.198) | copy-start | bytes 1572868
  133.0 17.8 %copy-start.14 = (f32[256,512]{1,0:T(8,128)}, f32[256,512]{1,0:T(8,128)S(1)}, u32[]{:S(2)}) copy-start(f32[256,512]{1,0:T(8,128)S(1)} %get-tuple-element.200) | copy-start | bytes 1572868
  133.0 17.8 %copy-start.18 = (f32[256,512]{1,0:T(8,128)}, f32[256,512]{1,0:T(8,128)S(1)}, u32[]{:S(2)}) copy-start(f32[256,512]{1,0:T(8,128)S(1)} %get-tuple-element.201) | copy-start | bytes 1572868
  133.0 17.8 %copy-start.22 = (f32[256,512]{1,0:T(8,128)}, f32[256,512]{1,0:T(8,128)S(1)}, u32[]{:S(2)}) copy-start(f32[256,512]{1,0:T(8,128)S(1)} %get-tuple-element.202) | copy-start | bytes 1572868
  133.0 17.8 %copy-start.39 = (f32[256,512]{1,0:T(8,128)}, f32[256,512]{1,0:T(8,128)S(1)}, u32[]{:S(2)}) copy-start(f32[256,512]{1,0:T(8,128)S(1)} %get-tuple-element.203) | copy-start | bytes 1572868
  133.0 15.3 %copy-start.10 = (f32[256,512]{1,0:T(8,128)S(1)}, f32[256,512]{1,0:T(8,128)}, u32[]{:S(2)}) copy-start(f32[256,512]{1,0:T(8,128)} %param.21) | copy-start | bytes 1572868
  133.1 5.7 %collective-permute-start.8 = (f32[1,512]{1,0:T(1,128)S(1)}, f32[1,512]{1,0:T(1,128)S(1)}, u32[]{:S(2)}, u32[]{:S(2)}) collective-permute-start(f32[1,512]{1,0:T(1,128)S(1)} %get-tuple-element.235), channel_id=1, source_target_pairs={{8,0},{16,8},{24,16},{32,24},{40,32},{48,40},{56,48},{64,56},{72,6... | collective-permute-start | bytes 6152 | tf_op jit(solution)/shard_map/ppermute | solution.py:21
  134.5 5.0 %collective-permute-start.9 = (f32[1,512]{1,0:T(1,128)S(1)}, f32[1,512]{1,0:T(1,128)S(1)}, u32[]{:S(2)}, u32[]{:S(2)}) collective-permute-start(f32[1,512]{1,0:T(1,128)S(1)} %get-tuple-element.234), channel_id=1, source_target_pairs={{0,8},{8,16},{16,24},{24,32},{32,40},{40,48},{48,56},{56,64},{64,7... | collective-permute-start | bytes 6152 | tf_op jit(solution)/shard_map/ppermute | solution.py:20
  139.6 7.2 %collective-permute-start.10 = (f32[258,1]{1,0:T(8,128)S(1)}, f32[258,1]{1,0:T(8,128)S(1)}, u32[]{:S(2)}, u32[]{:S(2)}) collective-permute-start(f32[258,1]{1,0:T(8,128)S(1)} %get-tuple-element.227), channel_id=1, source_target_pairs={{1,0},{2,1},{3,2},{4,3},{5,4},{6,5},{7,6},{9,8},{10,9},{11,10},{12... | collective-permute-start | bytes 3104 | tf_op jit(solution)/shard_map/ppermute | solution.py:21
  142.6 5.4 %collective-permute-start.11 = (f32[258,1]{1,0:T(8,128)S(1)}, f32[258,1]{1,0:T(8,128)S(1)}, u32[]{:S(2)}, u32[]{:S(2)}) collective-permute-start(f32[258,1]{1,0:T(8,128)S(1)} %get-tuple-element.226), channel_id=1, source_target_pairs={{0,1},{1,2},{2,3},{3,4},{4,5},{5,6},{6,7},{8,9},{9,10},{10,11},{11... | collective-permute-start | bytes 3104 | tf_op jit(solution)/shard_map/ppermute | solution.py:20
  228.6 18.4 %copy-start.6 = (f32[256,512]{1,0:T(8,128)}, f32[256,512]{1,0:T(8,128)S(1)}, u32[]{:S(2)}) copy-start(f32[256,512]{1,0:T(8,128)S(1)} %get-tuple-element.195) | copy-start | bytes 1572868
  228.6 18.4 %copy-start.41 = (f32[256,512]{1,0:T(8,128)}, f32[256,512]{1,0:T(8,128)S(1)}, u32[]{:S(2)}) copy-start(f32[256,512]{1,0:T(8,128)S(1)} %get-tuple-element.196) | copy-start | bytes 1572868
  228.6 15.9 %copy-start.11 = (f32[256,512]{1,0:T(8,128)S(1)}, f32[256,512]{1,0:T(8,128)}, u32[]{:S(2)}) copy-start(f32[256,512]{1,0:T(8,128)} %param.21) | copy-start | bytes 1572868
  228.6 15.9 %copy-start.15 = (f32[256,512]{1,0:T(8,128)S(1)}, f32[256,512]{1,0:T(8,128)}, u32[]{:S(2)}) copy-start(f32[256,512]{1,0:T(8,128)} %copy-done.14) | copy-start | bytes 1572868
  228.6 15.9 %copy-start.19 = (f32[256,512]{1,0:T(8,128)S(1)}, f32[256,512]{1,0:T(8,128)}, u32[]{:S(2)}) copy-start(f32[256,512]{1,0:T(8,128)} %copy-done.18) | copy-start | bytes 1572868
  228.6 15.9 %copy-start.23 = (f32[256,512]{1,0:T(8,128)S(1)}, f32[256,512]{1,0:T(8,128)}, u32[]{:S(2)}) copy-start(f32[256,512]{1,0:T(8,128)} %copy-done.22) | copy-start | bytes 1572868
  228.7 5.6 %collective-permute-start.12 = (f32[1,512]{1,0:T(1,128)S(1)}, f32[1,512]{1,0:T(1,128)S(1)}, u32[]{:S(2)}, u32[]{:S(2)}) collective-permute-start(f32[1,512]{1,0:T(1,128)S(1)} %get-tuple-element.233), channel_id=1, source_target_pairs={{8,0},{16,8},{24,16},{32,24},{40,32},{48,40},{56,48},{64,56},{72,6... | collective-permute-start | bytes 6152 | tf_op jit(solution)/shard_map/ppermute | solution.py:21
  230.2 4.7 collective-permute-start.13
  235.0 8.0 %collective-permute-start.14 = (f32[258,1]{1,0:T(8,128)S(1)}, f32[258,1]{1,0:T(8,128)S(1)}, u32[]{:S(2)}, u32[]{:S(2)}) collective-permute-start(f32[258,1]{1,0:T(8,128)S(1)} %get-tuple-element.223), channel_id=1, source_target_pairs={{1,0},{2,1},{3,2},{4,3},{5,4},{6,5},{7,6},{9,8},{10,9},{11,10},{12... | collective-permute-start | bytes 3104 | tf_op jit(solution)/shard_map/ppermute | solution.py:21
  238.7 5.5 %collective-permute-start.15 = (f32[258,1]{1,0:T(8,128)S(1)}, f32[258,1]{1,0:T(8,128)S(1)}, u32[]{:S(2)}, u32[]{:S(2)}) collective-permute-start(f32[258,1]{1,0:T(8,128)S(1)} %get-tuple-element.222), channel_id=1, source_target_pairs={{0,1},{1,2},{2,3},{3,4},{4,5},{5,6},{6,7},{8,9},{9,10},{10,11},{11... | collective-permute-start | bytes 3104 | tf_op jit(solution)/shard_map/ppermute | solution.py:20
  318.9 17.8 %copy-start.7 = (f32[256,512]{1,0:T(8,128)}, f32[256,512]{1,0:T(8,128)S(1)}, u32[]{:S(2)}) copy-start(f32[256,512]{1,0:T(8,128)S(1)} %get-tuple-element.191) | copy-start | bytes 1572868
  318.9 17.8 %copy-start.42 = (f32[256,512]{1,0:T(8,128)}, f32[256,512]{1,0:T(8,128)S(1)}, u32[]{:S(2)}) copy-start(f32[256,512]{1,0:T(8,128)S(1)} %get-tuple-element.192) | copy-start | bytes 1572868
  318.9 15.3 %copy-start.12 = (f32[256,512]{1,0:T(8,128)S(1)}, f32[256,512]{1,0:T(8,128)}, u32[]{:S(2)}) copy-start(f32[256,512]{1,0:T(8,128)} %param.21) | copy-start | bytes 1572868
  318.9 15.3 %copy-start.16 = (f32[256,512]{1,0:T(8,128)S(1)}, f32[256,512]{1,0:T(8,128)}, u32[]{:S(2)}) copy-start(f32[256,512]{1,0:T(8,128)} %copy-done.14) | copy-start | bytes 1572868
  319.0 15.3 %copy-start.20 = (f32[256,512]{1,0:T(8,128)S(1)}, f32[256,512]{1,0:T(8,128)}, u32[]{:S(2)}) copy-start(f32[256,512]{1,0:T(8,128)} %copy-done.18) | copy-start | bytes 1572868
  319.0 15.3 %copy-start.24 = (f32[256,512]{1,0:T(8,128)S(1)}, f32[256,512]{1,0:T(8,128)}, u32[]{:S(2)}) copy-start(f32[256,512]{1,0:T(8,128)} %copy-done.22) | copy-start | bytes 1572868
  319.0 5.6 %collective-permute-start.16 = (f32[1,512]{1,0:T(1,128)S(1)}, f32[1,512]{1,0:T(1,128)S(1)}, u32[]{:S(2)}, u32[]{:S(2)}) collective-permute-start(f32[1,512]{1,0:T(1,128)S(1)} %get-tuple-element.231), channel_id=1, source_target_pairs={{8,0},{16,8},{24,16},{32,24},{40,32},{48,40},{56,48},{64,56},{72,6... | collective-permute-start | bytes 6152 | tf_op jit(solution)/shard_map/ppermute | solution.py:21
  320.6 4.7 collective-permute-start.17
  325.4 7.4 %collective-permute-start.18 = (f32[258,1]{1,0:T(8,128)S(1)}, f32[258,1]{1,0:T(8,128)S(1)}, u32[]{:S(2)}, u32[]{:S(2)}) collective-permute-start(f32[258,1]{1,0:T(8,128)S(1)} %get-tuple-element.219), channel_id=1, source_target_pairs={{1,0},{2,1},{3,2},{4,3},{5,4},{6,5},{7,6},{9,8},{10,9},{11,10},{12... | collective-permute-start | bytes 3104 | tf_op jit(solution)/shard_map/ppermute | solution.py:21
  329.1 4.9 collective-permute-start.19
  408.3 17.1 %copy-start.8 = (f32[256,512]{1,0:T(8,128)}, f32[256,512]{1,0:T(8,128)S(1)}, u32[]{:S(2)}) copy-start(f32[256,512]{1,0:T(8,128)S(1)} %get-tuple-element.188) | copy-start | bytes 1572868
  408.3 17.1 %copy-start.40 = (f32[256,512]{1,0:T(8,128)}, f32[256,512]{1,0:T(8,128)S(1)}, u32[]{:S(2)}) copy-start(f32[256,512]{1,0:T(8,128)S(1)} %get-tuple-element.189) | copy-start | bytes 1572868
  408.3 14.6 %copy-start.13 = (f32[256,512]{1,0:T(8,128)S(1)}, f32[256,512]{1,0:T(8,128)}, u32[]{:S(2)}) copy-start(f32[256,512]{1,0:T(8,128)} %param.21) | copy-start | bytes 1572868
  408.3 14.6 %copy-start.17 = (f32[256,512]{1,0:T(8,128)S(1)}, f32[256,512]{1,0:T(8,128)}, u32[]{:S(2)}) copy-start(f32[256,512]{1,0:T(8,128)} %copy-done.14) | copy-start | bytes 1572868
  408.3 14.6 %copy-start.21 = (f32[256,512]{1,0:T(8,128)S(1)}, f32[256,512]{1,0:T(8,128)}, u32[]{:S(2)}) copy-start(f32[256,512]{1,0:T(8,128)} %copy-done.18) | copy-start | bytes 1572868
  408.3 14.6 %copy-start.25 = (f32[256,512]{1,0:T(8,128)S(1)}, f32[256,512]{1,0:T(8,128)}, u32[]{:S(2)}) copy-start(f32[256,512]{1,0:T(8,128)} %copy-done.22) | copy-start | bytes 1572868
  408.4 5.6 %collective-permute-start.20 = (f32[1,512]{1,0:T(1,128)S(1)}, f32[1,512]{1,0:T(1,128)S(1)}, u32[]{:S(2)}, u32[]{:S(2)}) collective-permute-start(f32[1,512]{1,0:T(1,128)S(1)} %get-tuple-element.229), channel_id=1, source_target_pairs={{8,0},{16,8},{24,16},{32,24},{40,32},{48,40},{56,48},{64,56},{72,6... | collective-permute-start | bytes 6152 | tf_op jit(solution)/shard_map/ppermute | solution.py:21
  409.9 4.7 collective-permute-start.21
  414.8 6.3 %collective-permute-start.22 = (f32[258,1]{1,0:T(8,128)S(1)}, f32[258,1]{1,0:T(8,128)S(1)}, u32[]{:S(2)}, u32[]{:S(2)}) collective-permute-start(f32[258,1]{1,0:T(8,128)S(1)} %get-tuple-element.215), channel_id=1, source_target_pairs={{1,0},{2,1},{3,2},{4,3},{5,4},{6,5},{7,6},{9,8},{10,9},{11,10},{12... | collective-permute-start | bytes 3104 | tf_op jit(solution)/shard_map/ppermute | solution.py:21
  418.7 3.9 collective-permute-start.23
  (5 other events, 8.8 us)
where the time goes:
time: 503 us; the launch traced here: 499 us
  blocking collectives  274 us (54%)
  other arithmetic  102 us (20%)
  starting transfers between devices  71.3 us (14%)
  local copies, waits for them, and re-layouts  27.6 us (5%)
  between operations  13.2 us (3%)
  waiting for transfers between devices  10.7 us (2%)
    psum x4, blocking collectives, chron_gear(): lax.psum((jnp.sum(residual * scaled), jnp.sum(scaled * applied)), ('blk',...  274 us
    ppermute x12, starting transfers between devices, padded_2(): before = lax.ppermute(last, axis, up)  42.8 us
    add x16, other arithmetic, add_level(): totals[1] + active * v_flow[level_index]  30.7 us
    add x16, other arithmetic, add_level(): totals[0] + active * u_flow[level_index]  29.4 us
    ppermute x12, starting transfers between devices, padded_2(): after = lax.ppermute(initial, axis, down)  28.4 us
    concatenate x10, other arithmetic, padded_2(): value = jnp.concatenate([before, value, after], axis=dim)  15.1 us
  transfers between devices with their start and end apart: 24, of which 12 were waited for; matrix products, arithmetic and copies ran while one was open for 19% of the time, Pallas kernels for 0%

commit v1 on v0

v1 whole, which is shorter than its diff:
```python
import jax
import jax.numpy as jnp
from jax import lax
from jax.experimental import pallas as pl
from jax.experimental.pallas import tpu as pltpu
from jax.sharding import PartitionSpec as P

F32 = jnp.float32
LEV = 16
LANES = 128
MESH = pl.DeviceIdType.MESH


def column_mask(shape):
    return lax.broadcasted_iota(jnp.int32, shape, 1)


def kernel(u, v, th_hbm, depth_hbm, ocean_hbm, cx_hbm, cy_hbm, cxy_hbm, cxm_hbm, ex_hbm, height, residual,
           ub, vb, dp, th, ocean, co, fl, w, sh, cen, minv, out,
           pack_c, pack_f, in_c, in_f, corner_c, corner_f, sums, msg,
           small_sem, coef_sem, flow_sem, send_c, recv_c, send_f, recv_f, send_s, recv_s, out_sem, know_x, know_y):
    rows, cols = dp.shape
    slabs = cols // LANES
    halo = slabs
    top, first, last = 8, 16, 16 + rows
    nblk, nsub = lax.axis_size("blk"), lax.axis_size("sub")
    blk, sub = lax.axis_index("blk"), lax.axis_index("sub")
    n_all = nblk * nsub
    ring = 4

    small = [
        pltpu.make_async_copy(depth_hbm, dp, small_sem.at[0]),
        pltpu.make_async_copy(th_hbm, th, small_sem.at[1]),
        pltpu.make_async_copy(ocean_hbm, ocean, small_sem.at[2]),
    ]
    for copy in small:
        copy.start()
    flows = []

    def flow_copy(r0, r1, c0, c1):
        for src, dst in ((u, ub), (v, vb)):
            copy = pltpu.make_async_copy(src.at[:, r0:r1, c0:c1], dst.at[:, r0:r1, c0:c1], flow_sem.at[len(flows)])
            copy.start()
            flows.append(copy)
        return flows[-2:]

    strips = [flow_copy(0, 8, 0, cols), flow_copy(rows - 8, rows, 0, cols)]
    coefs = []
    for a, src in enumerate((cx_hbm, cy_hbm, cxy_hbm, cxm_hbm, ex_hbm)):
        for s in range(slabs):
            copy = pltpu.make_async_copy(
                src.at[:, s * LANES:(s + 1) * LANES], co.at[a, s, first:last, :], coef_sem.at[a, s])
            copy.start()
            coefs.append(copy)
    half = rows // 2
    quarters = [(8, half // 2), (half // 2, half), (half, half + half // 2), (half + half // 2, rows - 8)]
    outer = [[flow_copy(r0, r1, 0, LANES), flow_copy(r0, r1, cols - LANES, cols)] for r0, r1 in quarters]
    middle = [[flow_copy(r0, r1, LANES, cols - LANES)] for r0, r1 in quarters]

    def near(db, ds):
        return (lax.rem(blk + db + nblk, nblk), lax.rem(sub + ds + nsub, nsub))

    def along_x(d):
        return (lax.rem(blk // ring + d, ring) * ring + lax.rem(blk, ring), sub)

    def along_y(d):
        return ((blk // ring) * ring + lax.rem(lax.rem(blk, ring) + d, ring), sub)

    greeted = [near(db, ds) for db in (-1, 1) for ds in (-1, 0, 1)]
    greeted += [near(0, d) for d in range(1, 8)]
    greeted += [along_x(d) for d in range(1, ring)] + [along_y(d) for d in range(1, ring)]
    barrier = pltpu.get_barrier_semaphore()
    for device in greeted:
        pl.semaphore_signal(barrier, inc=1, device_id=device, device_id_type=MESH)

    lane = lax.broadcasted_iota(jnp.int32, (8, LANES), 1)
    left_ok = (sub > 0).astype(F32)
    right_ok = (sub < nsub - 1).astype(F32)
    up_ok = (blk > 0).astype(F32)
    down_ok = (blk < nblk - 1).astype(F32)
    low = lane < 64
    side_ok = jnp.where(low, right_ok, left_ok)

    for copy in small:
        copy.wait()

    def mask_at(a, s):
        row = blk * 2 + a
        col = sub * slabs + s
        ok = 1.0
        if a < 0:
            row, ok = jnp.maximum(row, 0), ok * up_ok
        if a > 1:
            row, ok = jnp.minimum(row, 2 * nblk - 1), ok * down_ok
        if s < 0:
            col, ok = jnp.maximum(col, 0), ok * left_ok
        if s >= slabs:
            col, ok = jnp.minimum(col, slabs * nsub - 1), ok * right_ok
        return ocean[row, col].astype(F32) * ok

    def column_sums(r0, r1, slab_list, block):
        masks = [mask_at(block, s) for s in slab_list]

        def tile(t, carry):
            base = pl.multiple_of(r0 + t * 8, 8)
            for s, mask in zip(slab_list, masks):
                at = pl.ds(s * LANES, LANES)
                deep = dp[pl.ds(base, 8), at]
                total_u = jnp.zeros((8, LANES), F32)
                total_v = jnp.zeros((8, LANES), F32)
                for k in range(LEV):
                    active = jnp.where(deep > k, th[k], 0.0)
                    total_u = total_u + active * ub[k, pl.ds(base, 8), at]
                    total_v = total_v + active * vb[k, pl.ds(base, 8), at]
                fl[0, s, pl.ds(first + base, 8), :] = mask * total_u
                fl[1, s, pl.ds(first + base, 8), :] = mask * total_v
            return carry

        lax.fori_loop(0, (r1 - r0) // 8, tile, 0)

    for (r0, block), copies in zip(((0, 0), (rows - 8, 1)), strips):
        for copy in copies:
            copy.wait()
        column_sums(r0, r0 + 8, range(slabs), block)

    def pack(field, n, packed):
        for side, s, shift in ((0, 0, 0), (1, slabs - 1, 8)):
            for a in range(n):
                for h in range(2):
                    total = jnp.zeros((8, LANES), F32)
                    for g in range(16):
                        value = field[a, s, first + 16 * g + 8 * h:first + 16 * g + 8 * h + 8, :]
                        turn = (8 * g + shift) % LANES
                        if turn:
                            value = pltpu.roll(value, turn, 1)
                        total = jnp.where(lane // 8 == g, value, total)
                    packed[side, a, 8 * h:8 * h + 8, :] = total

    def unpack(field, n, arrived, corners):
        for a in range(n):
            inside = (lambda factor: 1.0) if a == 4 else (lambda factor: factor)
            for h in range(2):
                ahead = arrived[0, a, 8 * h:8 * h + 8, :]
                behind = arrived[1, a, 8 * h:8 * h + 8, :]
                for g in range(16):
                    right, left = ahead, behind
                    if g:
                        right = pltpu.roll(ahead, LANES - 8 * g, 1)
                    if g < 15:
                        left = pltpu.roll(behind, 120 - 8 * g, 1)
                    field[a, halo, first + 16 * g + 8 * h:first + 16 * g + 8 * h + 8, :] = (
                        inside(side_ok) * jnp.where(low, right, left))
            for row, ok, (right, left) in ((top, up_ok, (2, 3)), (last, down_ok, (0, 1))):
                field[a, halo, row:row + 8, :] = inside(side_ok * ok) * jnp.where(low, corners[right, a], corners[left, a])
                for s in range(slabs):
                    field[a, s, row:row + 8, :] = inside(ok) * field[a, s, row:row + 8, :]

    def row_sends(field, corners, send, recv):
        made = []
        for way, db, src, dst in ((0, -1, first, last), (1, 1, last - 8, top)):
            made.append(pltpu.make_async_remote_copy(
                src_ref=field.at[:, 0:slabs, src:src + 8, :], dst_ref=field.at[:, 0:slabs, dst:dst + 8, :],
                send_sem=send.at[way], recv_sem=recv.at[way], device_id=near(db, 0), device_id_type=MESH))
            for side, ds, s in ((0, -1, 0), (1, 1, slabs - 1)):
                slot = 2 * way + side
                made.append(pltpu.make_async_remote_copy(
                    src_ref=field.at[:, s, src:src + 8, :], dst_ref=corners.at[slot],
                    send_sem=send.at[2 + slot], recv_sem=recv.at[2 + slot],
                    device_id=near(db, ds), device_id_type=MESH))
        return made

    def side_sends(packed, arrived, send, recv):
        return [pltpu.make_async_remote_copy(
            src_ref=packed.at[side], dst_ref=arrived.at[side], send_sem=send.at[6 + side], recv_sem=recv.at[6 + side],
            device_id=near(0, ds), device_id_type=MESH) for side, ds in ((0, -1), (1, 1))]

    for copy in coefs:
        copy.wait()
    pack(co, 5, pack_c)

    pl.semaphore_wait(barrier, len(greeted))
    flux_sends = row_sends(fl, corner_f, send_f, recv_f)
    coef_sends = row_sends(co, corner_c, send_c, recv_c) + side_sends(pack_c, in_c, send_c, recv_c)
    for copy in coef_sends + flux_sends:
        copy.start()
    for d in range(1, ring):
        pl.semaphore_signal(know_x, inc=1, device_id=along_x(d), device_id_type=MESH)

    for q, (r0, r1) in enumerate(quarters):
        for copies in outer[q]:
            for copy in copies:
                copy.wait()
        column_sums(r0, r1, (0, slabs - 1), q // 2)
    pack(fl, 2, pack_f)
    more = side_sends(pack_f, in_f, send_f, recv_f)
    for copy in more:
        copy.start()
    flux_sends += more

    for q, (r0, r1) in enumerate(quarters):
        for copies in middle[q]:
            for copy in copies:
                copy.wait()
        column_sums(r0, r1, range(1, slabs - 1), q // 2)

    pl.semaphore_wait(know_x, ring - 1)
    for d in range(1, ring):
        pl.semaphore_signal(know_y, inc=1, device_id=along_y(d), device_id_type=MESH)

    every = range(slabs + 1)

    def from_next(values):
        turned = [pltpu.roll(value, LANES - 1, 1) for value in values]
        return [jnp.where(lane == LANES - 1, turned[(s + 1) % len(values)], turned[s]) for s in range(len(values))]

    def from_before(values):
        turned = [pltpu.roll(value, 1, 1) for value in values]
        return [jnp.where(lane == 0, turned[s - 1], turned[s]) for s in range(len(values))]

    for copy in coef_sends:
        copy.wait()
    unpack(co, 5, in_c, corner_c)

    def shift_tile(t, carry):
        at = pl.ds(pl.multiple_of(top + t * 8, 8), 8)
        for a, (src, turn) in enumerate(((1, from_before), (2, from_before), (3, from_next))):
            for s, value in enumerate(turn([co[src, s, at, :] for s in every])):
                sh[a, s, at, :] = value
        return carry

    lax.fori_loop(0, rows // 8 + 2, shift_tile, 0)

    def centres(t0, t1, block):
        masks = [mask_at(block, s) for s in range(slabs)]
        masks.append(jnp.where(low, mask_at(block, slabs), mask_at(block, -1)))

        def tile(t, carry):
            base = pl.multiple_of(top + t * 8, 8)
            at, above = pl.ds(base, 8), pl.ds(base - 1, 8)
            for s in every:
                total = co[4, s, at, :] + co[0, s, at, :] + co[0, s, above, :]
                total = total + co[1, s, at, :] + sh[0, s, at, :]
                total = total + co[2, s, at, :] + sh[1, s, above, :]
                total = total + co[3, s, at, :] + sh[2, s, above, :]
                cen[s, at, :] = total
                minv[s, at, :] = masks[s] / total
            return carry

        lax.fori_loop(t0, t1, tile, 0)

    tiles = rows // 8
    centres(0, 1, -1)
    centres(1, 1 + tiles // 2, 0)
    centres(1 + tiles // 2, 1 + tiles, 1)
    centres(1 + tiles, 2 + tiles, 2)

    for copy in flux_sends:
        copy.wait()
    unpack(fl, 2, in_f, corner_f)

    def over_tiles(tile, count):
        tile(top, False)
        tile(last, False)

        def step(t, totals):
            more = tile(pl.multiple_of(first + t * 8, 8), True)
            return tuple(a + b for a, b in zip(totals, more))

        return lax.fori_loop(0, tiles, step, tuple(jnp.zeros((8, LANES), F32) for _ in range(count)))

    def dot(left, right):
        total = left[0] * right[0]
        for s in range(1, slabs):
            total = total + left[s] * right[s]
        return total

    def forcing_tile(base, own):
        at, above, below = pl.ds(base, 8), pl.ds(base - 1, 8), pl.ds(base + 1, 8)
        across = [fl[1, s, at, :] for s in every]
        ahead, behind = from_next(across), from_before(across)
        force, start = [], []
        for s in every:
            value = 0.5 * ((fl[0, s, below, :] - fl[0, s, above, :]) + (ahead[s] - behind[s]))
            force.append(value)
            start.append(minv[s, at, :] * value)
            w[0, s, at, :] = start[s]
        return (dot(force, start),)

    moments = list(over_tiles(forcing_tile, 1))

    def apply_tile(j, end):
        def tile(base, own):
            at, above, below = pl.ds(base, 8), pl.ds(base - 1, 8), pl.ds(base + 1, 8)
            ahead, behind, beside, here = [], [], [], []
            for s in every:
                up, mid, down = w[j, s, above, :], w[j, s, at, :], w[j, s, below, :]
                ahead.append(sh[0, s, at, :] * mid + sh[1, s, at, :] * down + co[3, s, above, :] * up)
                behind.append(co[1, s, at, :] * mid + co[2, s, above, :] * up + sh[2, s, at, :] * down)
                beside.append(co[0, s, at, :] * down + co[0, s, above, :] * up)
                here.append(mid)
            ahead, behind = from_next(ahead), from_before(behind)
            total, after = [], []
            for s in range(slabs if end else slabs + 1):
                total.append(beside[s] + ahead[s] + behind[s])
                after.append(minv[s, at, :] * total[s])
                w[j + 1, s, at, :] = after[s]
            if end:
                return (dot(total, here),)
            return (dot(total, here), dot(total, after))
        return tile

    for j in range(3):
        moments += over_tiles(apply_tile(j, False), 2)
    final = apply_tile(3, True)
    moments += lax.fori_loop(
        0, tiles, lambda t, totals: (totals[0] + final(pl.multiple_of(first + t * 8, 8), True)[0],),
        (jnp.zeros((8, LANES), F32),))

    line = jnp.zeros((1, LANES), F32)
    lane_1 = lax.broadcasted_iota(jnp.int32, (1, LANES), 1)
    for k, moment in enumerate(moments):
        number = jnp.sum(jnp.sum(moment, axis=0, keepdims=True), axis=1, keepdims=True)
        line = jnp.where(lane_1 == k, number, line)
    msg[...] = line
    pl.semaphore_wait(know_y, ring - 1)
    me = blk * nsub + sub

    def send(d, carry):
        other = lax.rem(me + d, n_all)
        pltpu.make_async_remote_copy(
            src_ref=msg, dst_ref=sums.at[d - 1], send_sem=send_s, recv_sem=recv_s,
            device_id=(other // nsub, lax.rem(other, nsub)), device_id_type=MESH).start()
        return carry

    lax.fori_loop(1, n_all, send, 0)
    whole = pltpu.make_async_remote_copy(
        src_ref=sums, dst_ref=sums, send_sem=send_s, recv_sem=recv_s, device_id=near(0, 1), device_id_type=MESH)
    whole.wait_recv()
    whole.wait_send()
    line = line + jnp.sum(sums[...], axis=0)
    m = [jnp.broadcast_to(line[:, k:k + 1], (8, LANES)) for k in range(8)]

    def inner(left, right):
        parts = [None] * (len(left) + len(right) - 1)
        for i, a in enumerate(left):
            for j, b in enumerate(right):
                parts[i + j] = a * b if parts[i + j] is None else parts[i + j] + a * b
        total = parts[0] * m[0]
        for k in range(1, len(parts)):
            total = total + parts[k] * m[k]
        return total

    def plus(left, factor, right):
        out_ = list(left)
        for i, b in enumerate(right):
            if i < len(out_):
                out_[i] = out_[i] + factor * b
            else:
                out_.append(factor * b)
        return out_

    one = jnp.ones((8, LANES), F32)
    res, search, image, high = [one], [], [], []
    rho_old = sigma = None
    for iteration in range(4):
        applied = plus(res + [jnp.zeros((8, LANES), F32)], -1.0, [jnp.zeros((8, LANES), F32)] + res)
        rho = inner(res, res)
        curvature = inner(res, applied)
        if iteration == 0:
            sigma, search, image = curvature, res, applied
        else:
            beta = rho / rho_old
            sigma = curvature - beta * beta * sigma
            search = plus(res, beta, search)
            image = plus(applied, beta, image)
        alpha = rho / sigma
        rho_old = rho
        high = plus(high, alpha, search)
        res = plus(res, -alpha, image)

    def combine(t, carry):
        base = pl.multiple_of(t * 8, 8)
        at = pl.ds(first + base, 8)
        for s in range(slabs):
            value = w[0, s, at, :]
            total_h, total_r = high[0] * value, res[0] * value
            for j in range(1, 4):
                value = w[j, s, at, :]
                total_h = total_h + high[j] * value
                total_r = total_r + res[j] * value
            total_r = total_r + res[4] * w[4, s, at, :]
            out[0, pl.ds(base, 8), s * LANES:(s + 1) * LANES] = total_h
            out[1, pl.ds(base, 8), s * LANES:(s + 1) * LANES] = total_r * cen[s, at, :]
        return carry

    ends = []
    for part in range(4):
        lax.fori_loop(part * tiles // 4, (part + 1) * tiles // 4, combine, 0)
        r0, r1 = part * rows // 4, (part + 1) * rows // 4
        for i, dst in enumerate((height, residual)):
            copy = pltpu.make_async_copy(out.at[i, r0:r1, :], dst.at[r0:r1, :], out_sem.at[part, i])
            copy.start()
            ends.append(copy)
    for copy in ends:
        copy.wait()


def body(*args):
    rows, cols = args[3].shape
    tall = rows + 32
    slabs = cols // LANES
    n_all = lax.axis_size("blk") * lax.axis_size("sub")
    any_ = pl.BlockSpec(memory_space=pl.ANY)
    dma = pltpu.SemaphoreType.DMA
    field = lambda *lead: pltpu.VMEM((*lead, slabs + 1, tall, LANES), F32)
    scratch = [
        pltpu.VMEM((LEV, rows, cols), F32), pltpu.VMEM((LEV, rows, cols), F32), pltpu.VMEM((rows, cols), jnp.int32),
        pltpu.SMEM((LEV,), F32), pltpu.SMEM(args[4].shape, jnp.int32),
        field(5), field(2), field(5), field(3), field(), field(), pltpu.VMEM((2, rows, cols), F32),
        pltpu.VMEM((2, 5, 16, LANES), F32), pltpu.VMEM((2, 2, 16, LANES), F32),
        pltpu.VMEM((2, 5, 16, LANES), F32), pltpu.VMEM((2, 2, 16, LANES), F32),
        pltpu.VMEM((4, 5, 8, LANES), F32), pltpu.VMEM((4, 2, 8, LANES), F32),
        pltpu.VMEM((n_all - 1, 1, LANES), F32), pltpu.VMEM((1, LANES), F32),
        dma((3,)), dma((5, slabs)), dma((28,)), dma((8,)), dma((8,)), dma((8,)), dma((8,)), dma, dma, dma((4, 2)),
        pltpu.SemaphoreType.REGULAR, pltpu.SemaphoreType.REGULAR,
    ]
    shape = jax.ShapeDtypeStruct((rows, cols), F32)
    return pl.pallas_call(
        kernel, out_shape=(shape, shape), in_specs=[any_] * 10, out_specs=(any_, any_), scratch_shapes=scratch,
        compiler_params=pltpu.CompilerParams(
            collective_id=0, has_side_effects=True, vmem_limit_bytes=56 * 1024 * 1024),
        cost_estimate=pl.CostEstimate(flops=20_000_000, bytes_accessed=20_000_000, transcendentals=0),
    )(*args)


def solution(mesh):
    tile = P("blk", "sub")
    flow = P(None, "blk", "sub")
    return jax.shard_map(
        body, mesh=mesh,
        in_specs=(flow, flow, P(), tile, P(), tile, tile, tile, tile, tile),
        out_specs=(tile, tile), check_vma=False)
```

time: 503 us -> 49 us (0.10)
  blocking collectives: 274 us -> 0 us
  other arithmetic: 102 us -> 0 us
  starting transfers between devices: 71.3 us -> 0 us
  Pallas kernels: 0 us -> 44.4 us
  local copies, waits for them, and re-layouts: 27.6 us -> 3.74 us
  between operations: 13.2 us -> 0.64 us
  waiting for transfers between devices: 10.7 us -> 0 us
    psum x4 -> x0, blocking collectives: 274 us -> none  [chron_gear(): lax.psum((jnp.sum(residual * scaled), jnp.sum(scaled * applied)), ('blk',...]
    ppermute x24 -> x0, starting transfers between devices: 71.3 us -> none  [the longest x12 42.8 us: padded_2(): before = lax.ppermute(last, axis, up)]
    add x32 -> x0, other arithmetic: 60.1 us -> none  [the longest x16 30.7 us: add_level(): totals[1] + active * v_flow[level_index]]
    pallas_call x0 -> x1, Pallas kernels: none -> 44.4 us  [body(): pl.pallas_call(kernel, out_shape=(shape, shape), in_specs=[any_] * 10, ou...]
    concatenate x10 -> x0, other arithmetic: 15.1 us -> none  [padded_2(): value = jnp.concatenate([before, value, after], axis=dim)]
    ppermute x24 -> x0, waiting for transfers between devices: 10.7 us -> none  [the longest x12 8 us: padded_2(): before = lax.ppermute(last, axis, up)]
    reduce_sum x4 -> x0, other arithmetic: 9.76 us -> none  [chron_gear(): jnp.sum(scaled * applied)]
    mul x4 -> x0, other arithmetic: 9.68 us -> none  [chron_gear(): scaled = residual * inverse]
  transfers between devices with their start and end apart: 24 -> 0, of which waited for: 12 -> 0; matrix products, arithmetic and copies ran while one was open for 19% -> 0% of each run, Pallas kernels for 0% -> 0%
where the time goes in v1:
time: 49 us; the launch traced here: 48.8 us
  Pallas kernels  44.4 us (91%)
  local copies, waits for them, and re-layouts  3.74 us (8%)
  between operations  0.64 us (1%)
    pallas_call x1, Pallas kernels, body(): pl.pallas_call(kernel, out_shape=(shape, shape), in_specs=[any_] * 10, ou...  44.4 us
    unnamed x2, local copies, waits for them, and re-layouts  3.74 us

profile of v1, /device:TPU:1, one launch (start us, length us, event | category | flops | bytes accessed | tf_op | source)
XLA Modules:
  0.0 48.8 jit_solution(10507958765682833771)
XLA Ops:
  0.6 44.4 %shard_map.113 = (f32[256,512]{1,0:T(8,128)}, f32[256,512]{1,0:T(8,128)}) custom-call(f32[16,256,512]{2,1,0:T(8,128)} %u.1, f32[16,256,512]{2,1,0:T(8,128)} %v.1, f32[16]{0:T(128)} %th_hbm.1, s32[256,512]{1,0:T(8,128)} %depth_hbm.1, s32[32,32]{1,0:T(8,128)} %ocean_hbm.1, f32[256,512]{1,0:T(8,128)} %cx_hbm.1, f32[256,512]{1,0:T(8,128)} %cy_hbm.1, ...), custom_call_target="tpu_custom_call" | custom-call | flops 20000000 | bytes 20000000 | tf_op jit(solution)/shard_map/pallas_call | solution.py:428
  45.1 1.9 %copy.14 = f32[256,512]{1,0:T(8,128)} copy(f32[256,512]{1,0:T(8,128)} %get-tuple-element.4) | data formatting | bytes 1048576
  46.9 1.9 %copy.15 = f32[256,512]{1,0:T(8,128)} copy(f32[256,512]{1,0:T(8,128)} %get-tuple-element.5) | data formatting | bytes 1048576

commit v2 on v1

--- a/solution.py
+++ b/solution.py
@@ -8,6 +8,7 @@
 F32 = jnp.float32
 LEV = 16
 LANES = 128
+UNROLL = 8
 MESH = pl.DeviceIdType.MESH
 
 
@@ -15,18 +16,51 @@
     return lax.broadcasted_iota(jnp.int32, shape, 1)
 
 
-def kernel(u, v, th_hbm, depth_hbm, ocean_hbm, cx_hbm, cy_hbm, cxy_hbm, cxm_hbm, ex_hbm, height, residual,
-           ub, vb, dp, th, ocean, co, fl, w, sh, cen, minv, out,
+def kernel(u, v, th_hbm, depth_hbm, ocean_hbm, cx_hbm, cy_hbm, cxy_hbm, cxm_hbm, ex_hbm, w0, w1, w2, w3, w4, cen, mix,
+           ub, vb, dp, th, ocean, co, fl, sh, minv,
            pack_c, pack_f, in_c, in_f, corner_c, corner_f, sums, msg,
-           small_sem, coef_sem, flow_sem, send_c, recv_c, send_f, recv_f, send_s, recv_s, out_sem, know_x, know_y):
+           small_sem, coef_sem, flow_sem, send_c, recv_c, send_f, recv_f, send_s, recv_s, know_x, know_y):
     rows, cols = dp.shape
     slabs = cols // LANES
     halo = slabs
     top, first, last = 8, 16, 16 + rows
     nblk, nsub = lax.axis_size("blk"), lax.axis_size("sub")
     blk, sub = lax.axis_index("blk"), lax.axis_index("sub")
-    n_all = nblk * nsub
     ring = 4
+    w = (w0, w1, w2, w3, w4)
+
+    def near(db, ds):
+        return (blk + db, sub + ds)
+
+    def inside(db, ds):
+        row, col = blk + db, sub + ds
+        return (row >= 0) & (row < nblk) & (col >= 0) & (col < nsub)
+
+    def on_sub(d):
+        return (blk, lax.rem(sub + d, nsub))
+
+    def along_x(d):
+        return (lax.rem(blk // ring + d, ring) * ring + lax.rem(blk, ring), sub)
+
+    def along_y(d):
+        return ((blk // ring) * ring + lax.rem(lax.rem(blk, ring) + d, ring), sub)
+
+    barrier = pltpu.get_barrier_semaphore()
+    expected = 0
+    for db in (-1, 1):
+        for ds in (-1, 0, 1):
+            there = inside(db, ds)
+            expected = expected + there.astype(jnp.int32)
+
+            @pl.when(there)
+            def _(db=db, ds=ds):
+                pl.semaphore_signal(barrier, inc=1, device_id=near(db, ds), device_id_type=MESH)
+
+    greeted = [on_sub(d) for d in range(1, 8)]
+    greeted += [along_x(d) for d in range(1, ring)] + [along_y(d) for d in range(1, ring)]
+    for device in greeted:
+        pl.semaphore_signal(barrier, inc=1, device_id=device, device_id_type=MESH)
+    expected = expected + len(greeted)
 
     small = [
         pltpu.make_async_copy(depth_hbm, dp, small_sem.at[0]),
@@ -57,29 +91,13 @@
     outer = [[flow_copy(r0, r1, 0, LANES), flow_copy(r0, r1, cols - LANES, cols)] for r0, r1 in quarters]
     middle = [[flow_copy(r0, r1, LANES, cols - LANES)] for r0, r1 in quarters]
 
-    def near(db, ds):
-        return (lax.rem(blk + db + nblk, nblk), lax.rem(sub + ds + nsub, nsub))
-
-    def along_x(d):
-        return (lax.rem(blk // ring + d, ring) * ring + lax.rem(blk, ring), sub)
-
-    def along_y(d):
-        return ((blk // ring) * ring + lax.rem(lax.rem(blk, ring) + d, ring), sub)
-
-    greeted = [near(db, ds) for db in (-1, 1) for ds in (-1, 0, 1)]
-    greeted += [near(0, d) for d in range(1, 8)]
-    greeted += [along_x(d) for d in range(1, ring)] + [along_y(d) for d in range(1, ring)]
-    barrier = pltpu.get_barrier_semaphore()
-    for device in greeted:
-        pl.semaphore_signal(barrier, inc=1, device_id=device, device_id_type=MESH)
-
     lane = lax.broadcasted_iota(jnp.int32, (8, LANES), 1)
     left_ok = (sub > 0).astype(F32)
     right_ok = (sub < nsub - 1).astype(F32)
     up_ok = (blk > 0).astype(F32)
     down_ok = (blk < nblk - 1).astype(F32)
     low = lane < 64
-    side_ok = jnp.where(low, right_ok, left_ok)
+    side_in = jnp.where(low, right_ok, left_ok) > 0
 
     for copy in small:
         copy.wait()
@@ -116,7 +134,7 @@
                 fl[1, s, pl.ds(first + base, 8), :] = mask * total_v
             return carry
 
-        lax.fori_loop(0, (r1 - r0) // 8, tile, 0)
+        lax.fori_loop(0, (r1 - r0) // 8, tile, 0, unroll=min((r1 - r0) // 8, 2))
 
     for (r0, block), copies in zip(((0, 0), (rows - 8, 1)), strips):
         for copy in copies:
@@ -138,7 +156,7 @@
 
     def unpack(field, n, arrived, corners):
         for a in range(n):
-            inside = (lambda factor: 1.0) if a == 4 else (lambda factor: factor)
+            outside = 1.0 if a == 4 else 0.0
             for h in range(2):
                 ahead = arrived[0, a, 8 * h:8 * h + 8, :]
                 behind = arrived[1, a, 8 * h:8 * h + 8, :]
@@ -149,40 +167,50 @@
                     if g < 15:
                         left = pltpu.roll(behind, 120 - 8 * g, 1)
                     field[a, halo, first + 16 * g + 8 * h:first + 16 * g + 8 * h + 8, :] = (
-                        inside(side_ok) * jnp.where(low, right, left))
+                        jnp.where(side_in, jnp.where(low, right, left), outside))
             for row, ok, (right, left) in ((top, up_ok, (2, 3)), (last, down_ok, (0, 1))):
-                field[a, halo, row:row + 8, :] = inside(side_ok * ok) * jnp.where(low, corners[right, a], corners[left, a])
+                edge_in = jnp.broadcast_to(ok, lane.shape) > 0
+                field[a, halo, row:row + 8, :] = jnp.where(
+                    edge_in & side_in, jnp.where(low, corners[right, a], corners[left, a]), outside)
                 for s in range(slabs):
-                    field[a, s, row:row + 8, :] = inside(ok) * field[a, s, row:row + 8, :]
+                    field[a, s, row:row + 8, :] = jnp.where(edge_in, field[a, s, row:row + 8, :], outside)
 
     def row_sends(field, corners, send, recv):
         made = []
         for way, db, src, dst in ((0, -1, first, last), (1, 1, last - 8, top)):
-            made.append(pltpu.make_async_remote_copy(
+            made.append(((db, 0), pltpu.make_async_remote_copy(
                 src_ref=field.at[:, 0:slabs, src:src + 8, :], dst_ref=field.at[:, 0:slabs, dst:dst + 8, :],
-                send_sem=send.at[way], recv_sem=recv.at[way], device_id=near(db, 0), device_id_type=MESH))
+                send_sem=send.at[way], recv_sem=recv.at[way], device_id=near(db, 0), device_id_type=MESH)))
             for side, ds, s in ((0, -1, 0), (1, 1, slabs - 1)):
                 slot = 2 * way + side
-                made.append(pltpu.make_async_remote_copy(
+                made.append(((db, ds), pltpu.make_async_remote_copy(
                     src_ref=field.at[:, s, src:src + 8, :], dst_ref=corners.at[slot],
                     send_sem=send.at[2 + slot], recv_sem=recv.at[2 + slot],
-                    device_id=near(db, ds), device_id_type=MESH))
+                    device_id=near(db, ds), device_id_type=MESH)))
         return made
 
     def side_sends(packed, arrived, send, recv):
-        return [pltpu.make_async_remote_copy(
+        return [((0, ds), pltpu.make_async_remote_copy(
             src_ref=packed.at[side], dst_ref=arrived.at[side], send_sem=send.at[6 + side], recv_sem=recv.at[6 + side],
-            device_id=near(0, ds), device_id_type=MESH) for side, ds in ((0, -1), (1, 1))]
+            device_id=near(0, ds), device_id_type=MESH)) for side, ds in ((0, -1), (1, 1))]
+
+    def start_all(copies):
+        for (db, ds), copy in copies:
+            pl.when(inside(db, ds))(copy.start)
+
+    def finish_all(copies):
+        for (db, ds), copy in copies:
+            pl.when(inside(-db, -ds))(copy.wait_recv)
+            pl.when(inside(db, ds))(copy.wait_send)
 
     for copy in coefs:
         copy.wait()
     pack(co, 5, pack_c)
 
-    pl.semaphore_wait(barrier, len(greeted))
+    pl.semaphore_wait(barrier, expected)
     flux_sends = row_sends(fl, corner_f, send_f, recv_f)
     coef_sends = row_sends(co, corner_c, send_c, recv_c) + side_sends(pack_c, in_c, send_c, recv_c)
-    for copy in coef_sends + flux_sends:
-        copy.start()
+    start_all(coef_sends + flux_sends)
     for d in range(1, ring):
         pl.semaphore_signal(know_x, inc=1, device_id=along_x(d), device_id_type=MESH)
 
@@ -193,8 +221,7 @@
         column_sums(r0, r1, (0, slabs - 1), q // 2)
     pack(fl, 2, pack_f)
     more = side_sends(pack_f, in_f, send_f, recv_f)
-    for copy in more:
-        copy.start()
+    start_all(more)
     flux_sends += more
 
     for q, (r0, r1) in enumerate(quarters):
@@ -217,8 +244,7 @@
         turned = [pltpu.roll(value, 1, 1) for value in values]
         return [jnp.where(lane == 0, turned[s - 1], turned[s]) for s in range(len(values))]
 
-    for copy in coef_sends:
-        copy.wait()
+    finish_all(coef_sends)
     unpack(co, 5, in_c, corner_c)
 
     def shift_tile(t, carry):
@@ -228,7 +254,7 @@
                 sh[a, s, at, :] = value
         return carry
 
-    lax.fori_loop(0, rows // 8 + 2, shift_tile, 0)
+    lax.fori_loop(0, rows // 8 + 2, shift_tile, 0, unroll=2)
 
     def centres(t0, t1, block):
         masks = [mask_at(block, s) for s in range(slabs)]
@@ -246,7 +272,7 @@
                 minv[s, at, :] = masks[s] / total
             return carry
 
-        lax.fori_loop(t0, t1, tile, 0)
+        lax.fori_loop(t0, t1, tile, 0, unroll=min(t1 - t0, UNROLL))
 
     tiles = rows // 8
     centres(0, 1, -1)
@@ -254,8 +280,7 @@
     centres(1 + tiles // 2, 1 + tiles, 1)
     centres(1 + tiles, 2 + tiles, 2)
 
-    for copy in flux_sends:
-        copy.wait()
+    finish_all(flux_sends)
     unpack(fl, 2, in_f, corner_f)
 
     def over_tiles(tile, count):
@@ -266,7 +291,7 @@
             more = tile(pl.multiple_of(first + t * 8, 8), True)
             return tuple(a + b for a, b in zip(totals, more))
 
-        return lax.fori_loop(0, tiles, step, tuple(jnp.zeros((8, LANES), F32) for _ in range(count)))
+        return lax.fori_loop(0, tiles, step, tuple(jnp.zeros((8, LANES), F32) for _ in range(count)), unroll=UNROLL)
 
     def dot(left, right):
         total = left[0] * right[0]
@@ -283,7 +308,7 @@
             value = 0.5 * ((fl[0, s, below, :] - fl[0, s, above, :]) + (ahead[s] - behind[s]))
             force.append(value)
             start.append(minv[s, at, :] * value)
-            w[0, s, at, :] = start[s]
+            w[0][s, at, :] = start[s]
         return (dot(force, start),)
 
     moments = list(over_tiles(forcing_tile, 1))
@@ -293,7 +318,7 @@
             at, above, below = pl.ds(base, 8), pl.ds(base - 1, 8), pl.ds(base + 1, 8)
             ahead, behind, beside, here = [], [], [], []
             for s in every:
-                up, mid, down = w[j, s, above, :], w[j, s, at, :], w[j, s, below, :]
+                up, mid, down = w[j][s, above, :], w[j][s, at, :], w[j][s, below, :]
                 ahead.append(sh[0, s, at, :] * mid + sh[1, s, at, :] * down + co[3, s, above, :] * up)
                 behind.append(co[1, s, at, :] * mid + co[2, s, above, :] * up + sh[2, s, at, :] * down)
                 beside.append(co[0, s, at, :] * down + co[0, s, above, :] * up)
@@ -303,7 +328,7 @@
             for s in range(slabs if end else slabs + 1):
                 total.append(beside[s] + ahead[s] + behind[s])
                 after.append(minv[s, at, :] * total[s])
-                w[j + 1, s, at, :] = after[s]
+                w[j + 1][s, at, :] = after[s]
             if end:
                 return (dot(total, here),)
             return (dot(total, here), dot(total, after))
@@ -314,7 +339,7 @@
     final = apply_tile(3, True)
     moments += lax.fori_loop(
         0, tiles, lambda t, totals: (totals[0] + final(pl.multiple_of(first + t * 8, 8), True)[0],),
-        (jnp.zeros((8, LANES), F32),))
+        (jnp.zeros((8, LANES), F32),), unroll=UNROLL)
 
     line = jnp.zeros((1, LANES), F32)
     lane_1 = lax.broadcasted_iota(jnp.int32, (1, LANES), 1)
@@ -323,18 +348,18 @@
         line = jnp.where(lane_1 == k, number, line)
     msg[...] = line
     pl.semaphore_wait(know_y, ring - 1)
-    me = blk * nsub + sub
-
-    def send(d, carry):
-        other = lax.rem(me + d, n_all)
+    x_at = [lax.rem(blk // ring + d, ring) * ring for d in range(ring)]
+    y_at = [lax.rem(lax.rem(blk, ring) + d, ring) for d in range(ring)]
+    sub_at = [lax.rem(sub + d, nsub) for d in range(8)]
+    hops = (0, 1, 2, 1)
+    ways = [(dx, dy, ds) for dx in range(ring) for dy in range(ring) for ds in range(8) if dx or dy or ds]
+    ways.sort(key=lambda way: -hops[way[0]] - hops[way[1]] - hops[(way[2] + 1) // 2 % ring])
+    for slot, (dx, dy, ds) in enumerate(ways):
         pltpu.make_async_remote_copy(
-            src_ref=msg, dst_ref=sums.at[d - 1], send_sem=send_s, recv_sem=recv_s,
-            device_id=(other // nsub, lax.rem(other, nsub)), device_id_type=MESH).start()
-        return carry
-
-    lax.fori_loop(1, n_all, send, 0)
+            src_ref=msg, dst_ref=sums.at[slot], send_sem=send_s, recv_sem=recv_s,
+            device_id=(x_at[dx] + y_at[dy], sub_at[ds]), device_id_type=MESH).start()
     whole = pltpu.make_async_remote_copy(
-        src_ref=sums, dst_ref=sums, send_sem=send_s, recv_sem=recv_s, device_id=near(0, 1), device_id_type=MESH)
+        src_ref=sums, dst_ref=sums, send_sem=send_s, recv_sem=recv_s, device_id=on_sub(1), device_id_type=MESH)
     whole.wait_recv()
     whole.wait_send()
     line = line + jnp.sum(sums[...], axis=0)
@@ -378,24 +403,34 @@
         high = plus(high, alpha, search)
         res = plus(res, -alpha, image)
 
+    for i, value in enumerate(high + res):
+        mix[i] = value
+
+
+def finish(w0, w1, w2, w3, w4, cen, mix, height, residual, out, out_sem):
+    slabs, rows, first = cen.shape[0] - 1, out.shape[1], 16
+    tiles = rows // 8
+    high, res = [mix[i] for i in range(4)], [mix[4 + i] for i in range(5)]
+    fields = (w0, w1, w2, w3, w4)
+
     def combine(t, carry):
         base = pl.multiple_of(t * 8, 8)
         at = pl.ds(first + base, 8)
         for s in range(slabs):
-            value = w[0, s, at, :]
+            value = fields[0][s, at, :]
             total_h, total_r = high[0] * value, res[0] * value
             for j in range(1, 4):
-                value = w[j, s, at, :]
+                value = fields[j][s, at, :]
                 total_h = total_h + high[j] * value
                 total_r = total_r + res[j] * value
-            total_r = total_r + res[4] * w[4, s, at, :]
+            total_r = total_r + res[4] * fields[4][s, at, :]
             out[0, pl.ds(base, 8), s * LANES:(s + 1) * LANES] = total_h
             out[1, pl.ds(base, 8), s * LANES:(s + 1) * LANES] = total_r * cen[s, at, :]
         return carry
 
     ends = []
     for part in range(4):
-        lax.fori_loop(part * tiles // 4, (part + 1) * tiles // 4, combine, 0)
+        lax.fori_loop(part * tiles // 4, (part + 1) * tiles // 4, combine, 0, unroll=UNROLL)
         r0, r1 = part * rows // 4, (part + 1) * rows // 4
         for i, dst in enumerate((height, residual)):
             copy = pltpu.make_async_copy(out.at[i, r0:r1, :], dst.at[r0:r1, :], out_sem.at[part, i])
@@ -416,21 +451,29 @@
     scratch = [
         pltpu.VMEM((LEV, rows, cols), F32), pltpu.VMEM((LEV, rows, cols), F32), pltpu.VMEM((rows, cols), jnp.int32),
         pltpu.SMEM((LEV,), F32), pltpu.SMEM(args[4].shape, jnp.int32),
-        field(5), field(2), field(5), field(3), field(), field(), pltpu.VMEM((2, rows, cols), F32),
+        field(5), field(2), field(3), field(),
         pltpu.VMEM((2, 5, 16, LANES), F32), pltpu.VMEM((2, 2, 16, LANES), F32),
         pltpu.VMEM((2, 5, 16, LANES), F32), pltpu.VMEM((2, 2, 16, LANES), F32),
         pltpu.VMEM((4, 5, 8, LANES), F32), pltpu.VMEM((4, 2, 8, LANES), F32),
         pltpu.VMEM((n_all - 1, 1, LANES), F32), pltpu.VMEM((1, LANES), F32),
-        dma((3,)), dma((5, slabs)), dma((28,)), dma((8,)), dma((8,)), dma((8,)), dma((8,)), dma, dma, dma((4, 2)),
+        dma((3,)), dma((5, slabs)), dma((28,)), dma((8,)), dma((8,)), dma((8,)), dma((8,)), dma, dma,
         pltpu.SemaphoreType.REGULAR, pltpu.SemaphoreType.REGULAR,
     ]
+    vmem = pl.BlockSpec(memory_space=pltpu.VMEM)
+    middle = pl.pallas_call(
+        kernel, out_shape=[pltpu.VMEM((slabs + 1, tall, LANES), F32)] * 6 + [pltpu.VMEM((9, 8, LANES), F32)],
+        in_specs=[pl.BlockSpec(memory_space=pltpu.HBM)] * 10, out_specs=[vmem] * 7, scratch_shapes=scratch,
+        compiler_params=pltpu.CompilerParams(
+            collective_id=0, has_side_effects=True, vmem_limit_bytes=59 * 1024 * 1024),
+        cost_estimate=pl.CostEstimate(flops=20_000_000, bytes_accessed=20_000_000, transcendentals=0),
+    )(*args)
     shape = jax.ShapeDtypeStruct((rows, cols), F32)
     return pl.pallas_call(
-        kernel, out_shape=(shape, shape), in_specs=[any_] * 10, out_specs=(any_, any_), scratch_shapes=scratch,
-        compiler_params=pltpu.CompilerParams(
-            collective_id=0, has_side_effects=True, vmem_limit_bytes=56 * 1024 * 1024),
-        cost_estimate=pl.CostEstimate(flops=20_000_000, bytes_accessed=20_000_000, transcendentals=0),
-    )(*args)
+        finish, out_shape=(shape, shape), in_specs=[vmem] * 7, out_specs=(any_, any_),
+        scratch_shapes=[pltpu.VMEM((2, rows, cols), F32), dma((4, 2))],
+        compiler_params=pltpu.CompilerParams(vmem_limit_bytes=8 * 1024 * 1024),
+        cost_estimate=pl.CostEstimate(flops=2_000_000, bytes_accessed=1_000_000, transcendentals=0),
+    )(*middle)
 
 
 def solution(mesh):

time: 49 us -> 30 us (0.61)
  Pallas kernels: 44.4 us -> 29.3 us
  local copies, waits for them, and re-layouts: 3.74 us -> 0 us
    pallas_call x1 -> x2, Pallas kernels: 44.4 us -> 29.3 us  [the longest x1 28.2 us: body(): pl.pallas_call(kernel, out_shape=[pltpu.VMEM((slabs + 1, tall, LANES), F3...]
    unnamed x2 -> x0, local copies, waits for them, and re-layouts: 3.74 us -> none
where the time goes in v2:
time: 30 us; the launch traced here: 29.9 us
  Pallas kernels  29.3 us (98%)
  between operations  0.64 us (2%)
    pallas_call x1, Pallas kernels, body(): pl.pallas_call(kernel, out_shape=[pltpu.VMEM((slabs + 1, tall, LANES), F3...  28.2 us
    pallas_call x1, Pallas kernels, body(): pl.pallas_call(finish, out_shape=(shape, shape), in_specs=[vmem] * 7, out...  1.11 us

profile of v2, /device:TPU:1, one launch (start us, length us, event | category | flops | bytes accessed | tf_op | source)
XLA Modules:
  0.0 29.9 jit_solution(14547728501717706744)
XLA Ops:
  0.6 28.2 %shard_map.113 = (f32[5,288,128]{2,1,0:T(8,128)S(1)}, f32[5,288,128]{2,1,0:T(8,128)S(1)}, f32[5,288,128]{2,1,0:T(8,128)S(1)}, f32[5,288,128]{2,1,0:T(8,128)S(1)}...) custom-call(f32[16,256,512]{2,1,0:T(8,128)} %u.1, f32[16,256,512]{2,1,0:T(8,128)} %v.1, ...), custom_call_target="tpu_custom_call" | custom-call | flops 20000000 | bytes 20000000 | tf_op jit(solution)/shard_map/pallas_call | solution.py:463
  28.8 1.1 %shard_map.114 = (f32[256,512]{1,0:T(8,128)}, f32[256,512]{1,0:T(8,128)}) custom-call(f32[5,288,128]{2,1,0:T(8,128)S(1)} %get-tuple-element.9.w0, f32[5,288,128]{2,1,0:T(8,128)S(1)} %get-tuple-element.10.w1, f32[5,288,128]{2,1,0:T(8,128)S(1)} %get-tuple-element.11.w2, f32[5,288,128]{2,1,0:T(8,128)S(1)} %get-tuple-element.12.w3, ...), custom_call_target="tpu_custom_call" | custom-call | flops 2000000 | bytes 1000000 | tf_op jit(solution)/shard_map/pallas_call | solution.py:471

commit v3 on v2

--- a/solution.py
+++ b/solution.py
@@ -224,6 +224,58 @@
     start_all(more)
     flux_sends += more
 
+    every = range(slabs + 1)
+
+    def from_next(values):
+        turned = [pltpu.roll(value, LANES - 1, 1) for value in values]
+        return [jnp.where(lane == LANES - 1, turned[(s + 1) % len(values)], turned[s]) for s in range(len(values))]
+
+    def from_before(values):
+        turned = [pltpu.roll(value, 1, 1) for value in values]
+        return [jnp.where(lane == 0, turned[s - 1], turned[s]) for s in range(len(values))]
+
+    def shift_own(t, carry):
+        at = pl.ds(pl.multiple_of(first + t * 8, 8), 8)
+        for a, (src, turn, rim) in enumerate(((1, 1, 0), (2, 1, 0), (3, LANES - 1, LANES - 1))):
+            turned = [pltpu.roll(co[src, s, at, :], turn, 1) for s in range(slabs)]
+            step = 1 if rim == 0 else -1
+            for s in range(slabs):
+                before = s - step
+                sh[a, s, at, :] = jnp.where(lane == rim, turned[before], turned[s]) if 0 <= before < slabs else turned[s]
+            sh[a, halo, at, :] = turned[slabs - 1 if rim == 0 else 0]
+        return carry
+
+    def shift_halo(at):
+        for a, (src, turn, rim, edge) in enumerate(((1, 1, 0, 0), (2, 1, 0, 0), (3, LANES - 1, LANES - 1, slabs - 1))):
+            turned = pltpu.roll(co[src, halo, at, :], turn, 1)
+            sh[a, edge, at, :] = jnp.where(lane == rim, turned, sh[a, edge, at, :])
+            sh[a, halo, at, :] = jnp.where(lane == rim, sh[a, halo, at, :], turned)
+
+    def block_masks(block):
+        return [mask_at(block, s) for s in range(slabs)] + [
+            jnp.where(low, mask_at(block, slabs), mask_at(block, -1))]
+
+    masks_0, masks_1 = block_masks(0), block_masks(1)
+
+    def centre(base, slab_list, masks):
+        at, above = pl.ds(base, 8), pl.ds(base - 1, 8)
+        for s in slab_list:
+            total = co[4, s, at, :] + co[0, s, at, :] + co[0, s, above, :]
+            total = total + co[1, s, at, :] + sh[0, s, at, :]
+            total = total + co[2, s, at, :] + sh[1, s, above, :]
+            total = total + co[3, s, at, :] + sh[2, s, above, :]
+            cen[s, at, :] = total
+            minv[s, at, :] = masks[s] / total
+
+    def own_centres(t, carry):
+        masks = [jnp.where(t < tiles // 2, a, b) for a, b in zip(masks_0, masks_1)]
+        centre(pl.multiple_of(first + t * 8, 8), range(1, slabs - 1), masks)
+        return carry
+
+    tiles = rows // 8
+    lax.fori_loop(0, tiles, shift_own, 0, unroll=UNROLL)
+    lax.fori_loop(1, tiles, own_centres, 0, unroll=UNROLL)
+
     for q, (r0, r1) in enumerate(quarters):
         for copies in middle[q]:
             for copy in copies:
@@ -234,51 +286,27 @@
     for d in range(1, ring):
         pl.semaphore_signal(know_y, inc=1, device_id=along_y(d), device_id_type=MESH)
 
-    every = range(slabs + 1)
-
-    def from_next(values):
-        turned = [pltpu.roll(value, LANES - 1, 1) for value in values]
-        return [jnp.where(lane == LANES - 1, turned[(s + 1) % len(values)], turned[s]) for s in range(len(values))]
-
-    def from_before(values):
-        turned = [pltpu.roll(value, 1, 1) for value in values]
-        return [jnp.where(lane == 0, turned[s - 1], turned[s]) for s in range(len(values))]
-
     finish_all(coef_sends)
     unpack(co, 5, in_c, corner_c)
-
-    def shift_tile(t, carry):
-        at = pl.ds(pl.multiple_of(top + t * 8, 8), 8)
-        for a, (src, turn) in enumerate(((1, from_before), (2, from_before), (3, from_next))):
-            for s, value in enumerate(turn([co[src, s, at, :] for s in every])):
-                sh[a, s, at, :] = value
+    for edge in (top, last):
+        shift_own((edge - first) // 8, 0)
+        shift_halo(pl.ds(edge, 8))
+
+    def late_shift(t, carry):
+        shift_halo(pl.ds(pl.multiple_of(first + t * 8, 8), 8))
         return carry
 
-    lax.fori_loop(0, rows // 8 + 2, shift_tile, 0, unroll=2)
-
-    def centres(t0, t1, block):
-        masks = [mask_at(block, s) for s in range(slabs)]
-        masks.append(jnp.where(low, mask_at(block, slabs), mask_at(block, -1)))
-
-        def tile(t, carry):
-            base = pl.multiple_of(top + t * 8, 8)
-            at, above = pl.ds(base, 8), pl.ds(base - 1, 8)
-            for s in every:
-                total = co[4, s, at, :] + co[0, s, at, :] + co[0, s, above, :]
-                total = total + co[1, s, at, :] + sh[0, s, at, :]
-                total = total + co[2, s, at, :] + sh[1, s, above, :]
-                total = total + co[3, s, at, :] + sh[2, s, above, :]
-                cen[s, at, :] = total
-                minv[s, at, :] = masks[s] / total
-            return carry
-
-        lax.fori_loop(t0, t1, tile, 0, unroll=min(t1 - t0, UNROLL))
-
-    tiles = rows // 8
-    centres(0, 1, -1)
-    centres(1, 1 + tiles // 2, 0)
-    centres(1 + tiles // 2, 1 + tiles, 1)
-    centres(1 + tiles, 2 + tiles, 2)
+    lax.fori_loop(0, tiles, late_shift, 0, unroll=UNROLL)
+    centre(top, every, block_masks(-1))
+    centre(first, every, masks_0)
+    centre(last, every, block_masks(2))
+
+    def late_centres(t, carry):
+        masks = [jnp.where(t < tiles // 2, a, b) for a, b in zip(masks_0, masks_1)]
+        centre(pl.multiple_of(first + t * 8, 8), (0, slabs - 1, halo), masks)
+        return carry
+
+    lax.fori_loop(1, tiles, late_centres, 0, unroll=UNROLL)
 
     finish_all(flux_sends)
     unpack(fl, 2, in_f, corner_f)
@@ -347,6 +375,8 @@
         number = jnp.sum(jnp.sum(moment, axis=0, keepdims=True), axis=1, keepdims=True)
         line = jnp.where(lane_1 == k, number, line)
     msg[...] = line
+    n_all = nblk * nsub
+    sums[n_all - 1:n_all, :] = jnp.zeros((1, LANES), F32)
     pl.semaphore_wait(know_y, ring - 1)
     x_at = [lax.rem(blk // ring + d, ring) * ring for d in range(ring)]
     y_at = [lax.rem(lax.rem(blk, ring) + d, ring) for d in range(ring)]
@@ -356,13 +386,13 @@
     ways.sort(key=lambda way: -hops[way[0]] - hops[way[1]] - hops[(way[2] + 1) // 2 % ring])
     for slot, (dx, dy, ds) in enumerate(ways):
         pltpu.make_async_remote_copy(
-            src_ref=msg, dst_ref=sums.at[slot], send_sem=send_s, recv_sem=recv_s,
+            src_ref=msg, dst_ref=sums.at[slot:slot + 1, :], send_sem=send_s, recv_sem=recv_s,
             device_id=(x_at[dx] + y_at[dy], sub_at[ds]), device_id_type=MESH).start()
     whole = pltpu.make_async_remote_copy(
-        src_ref=sums, dst_ref=sums, send_sem=send_s, recv_sem=recv_s, device_id=on_sub(1), device_id_type=MESH)
+        src_ref=sums.at[0:n_all - 1, :], dst_ref=sums.at[0:n_all - 1, :], send_sem=send_s, recv_sem=recv_s, device_id=on_sub(1), device_id_type=MESH)
     whole.wait_recv()
     whole.wait_send()
-    line = line + jnp.sum(sums[...], axis=0)
+    line = line + jnp.sum(sums[0:n_all, :], axis=0, keepdims=True)
     m = [jnp.broadcast_to(line[:, k:k + 1], (8, LANES)) for k in range(8)]
 
     def inner(left, right):
@@ -455,7 +485,7 @@
         pltpu.VMEM((2, 5, 16, LANES), F32), pltpu.VMEM((2, 2, 16, LANES), F32),
         pltpu.VMEM((2, 5, 16, LANES), F32), pltpu.VMEM((2, 2, 16, LANES), F32),
         pltpu.VMEM((4, 5, 8, LANES), F32), pltpu.VMEM((4, 2, 8, LANES), F32),
-        pltpu.VMEM((n_all - 1, 1, LANES), F32), pltpu.VMEM((1, LANES), F32),
+        pltpu.VMEM((n_all, LANES), F32), pltpu.VMEM((1, LANES), F32),
         dma((3,)), dma((5, slabs)), dma((28,)), dma((8,)), dma((8,)), dma((8,)), dma((8,)), dma, dma,
         pltpu.SemaphoreType.REGULAR, pltpu.SemaphoreType.REGULAR,
     ]

time: 30 us -> 28.5 us (0.950)
  Pallas kernels: 29.3 us -> 27.8 us
    pallas_call x1, Pallas kernels: 28.2 us -> 26.7 us  [body(): pl.pallas_call(kernel, out_shape=[pltpu.VMEM((slabs + 1, tall, LANES), F3...]
where the time goes in v3:
time: 28.5 us; the launch traced here: 28.4 us
  Pallas kernels  27.8 us (98%)
  between operations  0.64 us (2%)
    pallas_call x1, Pallas kernels, body(): pl.pallas_call(kernel, out_shape=[pltpu.VMEM((slabs + 1, tall, LANES), F3...  26.7 us
    pallas_call x1, Pallas kernels, body(): pl.pallas_call(finish, out_shape=(shape, shape), in_specs=[vmem] * 7, out...  1.11 us

profile of v3, /device:TPU:1, one launch (start us, length us, event | category | flops | bytes accessed | tf_op | source)
XLA Modules:
  0.0 28.4 jit_solution(4808654174972516822)
XLA Ops:
  0.6 26.7 %shard_map.113 = (f32[5,288,128]{2,1,0:T(8,128)S(1)}, f32[5,288,128]{2,1,0:T(8,128)S(1)}, f32[5,288,128]{2,1,0:T(8,128)S(1)}, f32[5,288,128]{2,1,0:T(8,128)S(1)}...) custom-call(f32[16,256,512]{2,1,0:T(8,128)} %u.1, f32[16,256,512]{2,1,0:T(8,128)} %v.1, ...), custom_call_target="tpu_custom_call" | custom-call | flops 20000000 | bytes 20000000 | tf_op jit(solution)/shard_map/pallas_call | solution.py:493
  27.3 1.1 %shard_map.114 = (f32[256,512]{1,0:T(8,128)}, f32[256,512]{1,0:T(8,128)}) custom-call(f32[5,288,128]{2,1,0:T(8,128)S(1)} %get-tuple-element.9.w0, f32[5,288,128]{2,1,0:T(8,128)S(1)} %get-tuple-element.10.w1, f32[5,288,128]{2,1,0:T(8,128)S(1)} %get-tuple-element.11.w2, f32[5,288,128]{2,1,0:T(8,128)S(1)} %get-tuple-element.12.w3, ...), custom_call_target="tpu_custom_call" | custom-call | flops 2000000 | bytes 1000000 | tf_op jit(solution)/shard_map/pallas_call | solution.py:501

commit v4 on v3

--- a/solution.py
+++ b/solution.py
@@ -319,7 +319,7 @@
             more = tile(pl.multiple_of(first + t * 8, 8), True)
             return tuple(a + b for a, b in zip(totals, more))
 
-        return lax.fori_loop(0, tiles, step, tuple(jnp.zeros((8, LANES), F32) for _ in range(count)), unroll=UNROLL)
+        return lax.fori_loop(0, tiles, step, tuple(jnp.zeros((8, LANES), F32) for _ in range(count)), unroll=tiles)
 
     def dot(left, right):
         total = left[0] * right[0]
@@ -367,7 +367,7 @@
     final = apply_tile(3, True)
     moments += lax.fori_loop(
         0, tiles, lambda t, totals: (totals[0] + final(pl.multiple_of(first + t * 8, 8), True)[0],),
-        (jnp.zeros((8, LANES), F32),), unroll=UNROLL)
+        (jnp.zeros((8, LANES), F32),), unroll=tiles)
 
     line = jnp.zeros((1, LANES), F32)
     lane_1 = lax.broadcasted_iota(jnp.int32, (1, LANES), 1)

time: 28.5 us -> 27.6 us (0.968)
  Pallas kernels: 27.8 us -> 26.8 us
    pallas_call x1, Pallas kernels: 26.7 us -> 25.7 us  [body(): pl.pallas_call(kernel, out_shape=[pltpu.VMEM((slabs + 1, tall, LANES), F3...]
where the time goes in v4:
time: 27.6 us; the launch traced here: 27.5 us
  Pallas kernels  26.8 us (97%)
  between operations  0.64 us (2%)
    pallas_call x1, Pallas kernels, body(): pl.pallas_call(kernel, out_shape=[pltpu.VMEM((slabs + 1, tall, LANES), F3...  25.7 us
    pallas_call x1, Pallas kernels, body(): pl.pallas_call(finish, out_shape=(shape, shape), in_specs=[vmem] * 7, out...  1.11 us

profile of v4, /device:TPU:1, one launch (start us, length us, event | category | flops | bytes accessed | tf_op | source)
XLA Modules:
  0.0 27.5 jit_solution(920656533272249411)
XLA Ops:
  0.6 25.7 %shard_map.113 = (f32[5,288,128]{2,1,0:T(8,128)S(1)}, f32[5,288,128]{2,1,0:T(8,128)S(1)}, f32[5,288,128]{2,1,0:T(8,128)S(1)}, f32[5,288,128]{2,1,0:T(8,128)S(1)}...) custom-call(f32[16,256,512]{2,1,0:T(8,128)} %u.1, f32[16,256,512]{2,1,0:T(8,128)} %v.1, ...), custom_call_target="tpu_custom_call" | custom-call | flops 20000000 | bytes 20000000 | tf_op jit(solution)/shard_map/pallas_call | solution.py:493
  26.4 1.1 %shard_map.114 = (f32[256,512]{1,0:T(8,128)}, f32[256,512]{1,0:T(8,128)}) custom-call(f32[5,288,128]{2,1,0:T(8,128)S(1)} %get-tuple-element.9.w0, f32[5,288,128]{2,1,0:T(8,128)S(1)} %get-tuple-element.10.w1, f32[5,288,128]{2,1,0:T(8,128)S(1)} %get-tuple-element.11.w2, f32[5,288,128]{2,1,0:T(8,128)S(1)} %get-tuple-element.12.w3, ...), custom_call_target="tpu_custom_call" | custom-call | flops 2000000 | bytes 1000000 | tf_op jit(solution)/shard_map/pallas_call | solution.py:501

commit v5 on v4

--- a/solution.py
+++ b/solution.py
@@ -210,7 +210,7 @@
     pl.semaphore_wait(barrier, expected)
     flux_sends = row_sends(fl, corner_f, send_f, recv_f)
     coef_sends = row_sends(co, corner_c, send_c, recv_c) + side_sends(pack_c, in_c, send_c, recv_c)
-    start_all(coef_sends + flux_sends)
+    start_all(sorted(coef_sends, key=lambda entry: -abs(entry[0][0]) - abs(entry[0][1])) + sorted(flux_sends, key=lambda entry: -abs(entry[0][0]) - abs(entry[0][1])))
     for d in range(1, ring):
         pl.semaphore_signal(know_x, inc=1, device_id=along_x(d), device_id_type=MESH)
 

time: 27.6 us -> 27.1 us (0.982)
  Pallas kernels: 26.8 us -> 26.4 us
    pallas_call x1, Pallas kernels: 25.7 us -> 25.3 us  [body(): pl.pallas_call(kernel, out_shape=[pltpu.VMEM((slabs + 1, tall, LANES), F3...]
where the time goes in v5:
time: 27.1 us; the launch traced here: 27 us
  Pallas kernels  26.4 us (97%)
  between operations  0.64 us (2%)
    pallas_call x1, Pallas kernels, body(): pl.pallas_call(kernel, out_shape=[pltpu.VMEM((slabs + 1, tall, LANES), F3...  25.3 us
    pallas_call x1, Pallas kernels, body(): pl.pallas_call(finish, out_shape=(shape, shape), in_specs=[vmem] * 7, out...  1.11 us

profile of v5, /device:TPU:1, one launch (start us, length us, event | category | flops | bytes accessed | tf_op | source)
XLA Modules:
  0.0 27.0 jit_solution(8088157689208723322)
XLA Ops:
  0.6 25.3 %shard_map.113 = (f32[5,288,128]{2,1,0:T(8,128)S(1)}, f32[5,288,128]{2,1,0:T(8,128)S(1)}, f32[5,288,128]{2,1,0:T(8,128)S(1)}, f32[5,288,128]{2,1,0:T(8,128)S(1)}...) custom-call(f32[16,256,512]{2,1,0:T(8,128)} %u.1, f32[16,256,512]{2,1,0:T(8,128)} %v.1, ...), custom_call_target="tpu_custom_call" | custom-call | flops 20000000 | bytes 20000000 | tf_op jit(solution)/shard_map/pallas_call | solution.py:493
  25.9 1.1 %shard_map.114 = (f32[256,512]{1,0:T(8,128)}, f32[256,512]{1,0:T(8,128)}) custom-call(f32[5,288,128]{2,1,0:T(8,128)S(1)} %get-tuple-element.9.w0, f32[5,288,128]{2,1,0:T(8,128)S(1)} %get-tuple-element.10.w1, f32[5,288,128]{2,1,0:T(8,128)S(1)} %get-tuple-element.11.w2, f32[5,288,128]{2,1,0:T(8,128)S(1)} %get-tuple-element.12.w3, ...), custom_call_target="tpu_custom_call" | custom-call | flops 2000000 | bytes 1000000 | tf_op jit(solution)/shard_map/pallas_call | solution.py:501
